TPU v7x, 32 devices: a whole 2x2x4 slice. The times are simulated.
32 devices in a mesh: occ: 4 (over y, x), vir: 4 (over z), rep: 2 (over core).
Axes of the slice: x: 2, y: 2, z: 4, core: 2. Of those that a mesh axis runs over, the one named last changes fastest.
Arguments:
- amplitudes: bfloat16 [2048, 4096], P('occ', 'vir'), may hold values from -6 to 6
- integrals: bfloat16 [8, 24, 512, 512], P('vir', 'rep'), may hold values from -0.0546875 to 0.0546875
- cd_tiles: int32 [8, 24], P('vir', 'rep'), may hold values from 0 to 7, as said below
- occ_energy: float32 [2048], P('occ'), may hold values from -2 to -0.5
- pair_energy: float32 [4096], P('vir'), may hold values from 0.5 to 3
Outputs:
- resid: bfloat16 [2048, 4096], P(('occ', 'rep'), 'vir')
Inputs may be any that keep to these rules, and one draw needn't show every extreme that they name: `cd_tiles`: every tile is named by some entry; a tile may be named more than once in a row.
All inputs are finite; a program needn't handle non-finite values.
Results may differ from a plain program's by a relative error of at most 0.007.
Values may be sent and summed in bfloat16 or wider, within the bound.
No kernel may reach another device: no remote copies, remote signals or barrier semaphores. Data moves between devices by JAX's collectives and lax.ppermute only.
A program may use at most 192 MiB of HBM per device.

v0:
```python
import jax
import jax.numpy as jnp
from jax import lax
from jax.sharding import PartitionSpec as P


def ladder_tiles(amp_rows, blocks, chosen, tile_width):
    row_count = amp_rows.shape[0]
    tile_view = amp_rows.reshape(row_count, -1, tile_width)
    picked = jnp.take(tile_view, chosen.reshape(-1), axis=1)
    picked = picked.reshape(row_count, chosen.shape[0], chosen.shape[1], tile_width)
    result = jnp.einsum("rakp,akpq->raq", picked, blocks, preferred_element_type=jnp.float32)
    return result.reshape(row_count, -1)


def local(amplitudes, integrals, cd_tiles, occ_energy, pair_energy):
    tile_width = integrals.shape[2]
    own_rows = amplitudes.shape[0]
    n_rep = lax.axis_size("rep")
    rep_rows = own_rows // n_rep
    rep_index = lax.axis_index("rep")
    own_amps = lax.dynamic_slice_in_dim(amplitudes, rep_index * rep_rows, rep_rows, 0)
    whole = lax.all_gather(amplitudes, "vir", axis=1, tiled=True)
    partial_value = ladder_tiles(whole, integrals, cd_tiles, tile_width)
    sums = lax.psum_scatter(
        partial_value.astype(jnp.bfloat16), "rep", scatter_dimension=0, tiled=True
    ).astype(jnp.float32)
    own_occ = lax.dynamic_slice_in_dim(occ_energy, rep_index * rep_rows, rep_rows, 0)
    energy_gap = pair_energy[None, :] - own_occ[:, None]
    return (sums + energy_gap * own_amps.astype(jnp.float32)).astype(jnp.bfloat16)


def solution(mesh):
    in_specs = (P("occ", "vir"), P("vir", "rep", None, None), P("vir", "rep"), P("occ"), P("vir"))
    out_specs = P(("occ", "rep"), "vir")
    return jax.shard_map(local, mesh=mesh, in_specs=in_specs, out_specs=out_specs, check_vma=False)
```

profile of v0, /device:TPU:18, one launch (start us, length us, event | category | flops | bytes accessed | tf_op | source)
XLA Modules:
  0.0 135.2 jit_solution(12770019207011708017)
XLA Ops:
  6.5 0.0 all-gather.2.cloned.1.call-start
  6.5 2.3 %copy.11 = bf16[512,1024]{0,1:T(8,128)(2,1)} copy(bf16[512,1024]{1,0:T(8,128)(2,1)} %param.5) | data formatting | bytes 2097152 | tf_op args[0]
  8.8 0.0 all-gather.2.cloned.1.call-update
  8.8 0.0 reduce-scatter.2.cloned.1.call-start
  8.9 0.8 reshape.48
  9.7 0.7 compare_and_fusion
  10.4 79.0 %all-gather.2.cloned.1.call-done = bf16[512,4096]{0,1:T(8,128)(2,1)} async-done(((bf16[512,1024]{0,1:T(8,128)(2,1)}), bf16[512,4096]{0,1:T(8,128)(2,1)}) %all-gather.2.cloned.1.call-update) | async-done | bytes 4194320 | tf_op jit(solution)/shard_map/all_gather | solution.py:23
  89.3 6.5 %copy.12 = bf16[512,8,512]{2,0,1:T(8,128)(2,1)} copy(bf16[512,8,512]{0,2,1:T(8,128)(2,1)} %bitcast.14) | data formatting | bytes 8388608 | tf_op jit(solution)/shard_map/reshape | solution.py:9
  95.8 8.2 %gather_fusion = bf16[24,512,512]{2,1,0:T(8,128)(2,1)} fusion(bf16[512,8,512]{2,0,1:T(8,128)(2,1)} %copy.12, s32[1024]{0:T(1024)S(1)} %pad_clamp_fusion), kind=kCustom, calls=%fused_computation | custom fusion | bytes 25165920 | tf_op jit(solution)/shard_map/jit(_take)/gather | solution.py:10
  104.1 0.0 copy-start.2
  104.1 0.0 copy-start
  104.1 0.0 copy-start.1
  104.1 11.9 %bitcast_convert_fusion = bf16[2,512,512]{1,2,0:T(8,128)(2,1)S(1)} fusion(bf16[2,12,512,512]{3,2,1,0:T(8,128)(2,1)} %param.6, bf16[512,2,12,512]{3,0,2,1:T(8,128)(2,1)} %bitcast.13, pred[2,12]{1,0:T(4,128)(4,1)S(1)} %compare_and_fusion), kind=kOutput, calls=%fused_computation.5 | convolution fusion | flops 6449266688 | bytes 26214424 | tf_op jit(solution)/shard_map/rakp,akpq->raq/dot_general | solution.py:12
  116.0 1.3 copy.14
  117.3 0.0 reduce-scatter.2.cloned.1.call-update
  117.4 0.0 copy-done.2
  117.4 0.1 dynamic_slice.6
  117.5 8.8 %reduce-scatter.2.cloned.1.call-done = bf16[256,1024]{1,0:T(8,128)(2,1)} async-done(((bf16[512,1024]{1,0:T(8,128)(2,1)}), bf16[256,1024]{1,0:T(8,128)(2,1)}) %reduce-scatter.2.cloned.1.call-update) | async-done | bytes 524304 | tf_op jit(solution)/shard_map/reduce_scatter | solution.py:25
  126.3 0.0 copy-done
  126.3 0.0 copy-done.1
  126.3 2.1 %add_convert_fusion = bf16[256,1024]{1,0:T(8,128)(2,1)} fusion(bf16[256,1024]{1,0:T(8,128)(2,1)} %reduce-scatter.2.cloned.1.call-done, bf16[512,1024]{1,0:T(8,128)(2,1)S(1)} %copy-done, s32[]{:T(128)S(6)} %select_n.29, f32[256]{0:T(256)S(1)} %dynamic_slice.6, f32[1024]{0:T(1024)S(1)} %copy-done.1), kind=kLoop, calls=%fused_computation.6 | loop fusion | flops 1572864 | bytes 1577988 | tf_op jit(solution)/shard_map/convert_element_type | solution.py:30
  (2 shorter events, 0.0 us)
Async XLA Ops:
  6.5 82.8 %all-gather.2.cloned.1.call-start = ((), (), s32[]{:S(2)}) async-start(), calls=%async_computation.1 | async-start | bytes 5242880 | tf_op jit(solution)/shard_map/all_gather | solution.py:23
  8.8 117.5 %reduce-scatter.2.cloned.1.call-start = ((), (), s32[]{:S(2)}) async-start(), calls=%async_computation.2 | async-start | bytes 1572864 | tf_op jit(solution)/shard_map/reduce_scatter | solution.py:25
  104.1 13.3 %copy-start.2 = (f32[512]{0:T(512)S(1)}, f32[512]{0:T(512)}, u32[]{:S(2)}) copy-start(f32[512]{0:T(512)} %param.8) | copy-start | bytes 6148
  104.1 22.2 %copy-start = (bf16[512,1024]{1,0:T(8,128)(2,1)S(1)}, bf16[512,1024]{1,0:T(8,128)(2,1)}, u32[]{:S(2)}) copy-start(bf16[512,1024]{1,0:T(8,128)(2,1)} %param.5) | copy-start | bytes 3145732
  104.1 22.2 %copy-start.1 = (f32[1024]{0:T(1024)S(1)}, f32[1024]{0:T(1024)}, u32[]{:S(2)}) copy-start(f32[1024]{0:T(1024)} %param.9) | copy-start | bytes 12292
Sparse Core Ops, SparseCore 0:
  9.0 80.3 all-gather.1
  117.5 8.7 reduce-scatter.1
where the time goes:
time: 137 us; the launch traced here: 135 us
  waiting for transfers between devices  87.9 us (64%)
  local copies, waits for them, and re-layouts  19.2 us (14%)
  between operations  13.4 us (10%)
  matrix products  11.9 us (9%)
  other arithmetic  2.79 us (2%)
    all_gather x1, waiting for transfers between devices, local(): whole = lax.all_gather(amplitudes, 'vir', axis=1, tiled=True)  79 us
    dot_general x1, matrix products, ladder_tiles(): jnp.einsum('rakp,akpq->raq', picked, blocks, preferred_element_type=jnp.f...  11.9 us
    reduce_scatter x1, waiting for transfers between devices, local(): lax.psum_scatter(partial_value.astype(jnp.bfloat16), 'rep', scatter_dimen...  8.85 us
    gather x1, local copies, waits for them, and re-layouts, ladder_tiles(): picked = jnp.take(tile_view, chosen.reshape(-1), axis=1)  8.23 us
    reshape x1, local copies, waits for them, and re-layouts, ladder_tiles(): tile_view = amp_rows.reshape(row_count, -1, tile_width)  6.49 us
  transfers between devices with their start and end apart: 2, of which 2 were waited for; matrix products, arithmetic and copies ran while one was open for 1% of the time, Pallas kernels for 0%

commit v1 on v0

--- a/solution.py
+++ b/solution.py
@@ -1,7 +1,13 @@
+import functools
+
 import jax
 import jax.numpy as jnp
 from jax import lax
+from jax.experimental import pallas as pl
+from jax.experimental.pallas import tpu as pltpu
 from jax.sharding import PartitionSpec as P
+
+MIB = 1024 * 1024
 
 
 def ladder_tiles(amp_rows, blocks, chosen, tile_width):
@@ -13,11 +19,10 @@
     return result.reshape(row_count, -1)
 
 
-def local(amplitudes, integrals, cd_tiles, occ_energy, pair_energy):
+def sparse_local(amplitudes, integrals, cd_tiles, occ_energy, pair_energy):
     tile_width = integrals.shape[2]
     own_rows = amplitudes.shape[0]
-    n_rep = lax.axis_size("rep")
-    rep_rows = own_rows // n_rep
+    rep_rows = own_rows // lax.axis_size("rep")
     rep_index = lax.axis_index("rep")
     own_amps = lax.dynamic_slice_in_dim(amplitudes, rep_index * rep_rows, rep_rows, 0)
     whole = lax.all_gather(amplitudes, "vir", axis=1, tiled=True)
@@ -30,7 +35,403 @@
     return (sums + energy_gap * own_amps.astype(jnp.float32)).astype(jnp.bfloat16)
 
 
+ARRIVAL = ((0, 1, 2, 3), (1, 0, 2, 3), (2, 3, 1, 0), (3, 2, 1, 0))
+PIECES = 2
+STEP = 128
+MOST = 4
+
+
+def arrival_of(vir_index, place):
+    chunk = jnp.int32(0)
+    for index, chunks in enumerate(ARRIVAL):
+        chunk = jnp.where(vir_index == index, chunks[place], chunk)
+    return chunk
+
+
+def list_entries(vir_index, sources, count_ref, entry_ref, per, n_held):
+    n_place = len(ARRIVAL[0])
+    places = [jnp.int32(0)] * n_place
+    for place in range(n_place):
+        for chunk in range(n_place):
+            places[chunk] = jnp.where(arrival_of(vir_index, place) == chunk, place, places[chunk])
+
+    @pl.loop(0, count_ref.shape[0])
+    def _(s):
+        count_ref[s] = 0
+
+    for chosen_ref, a, i, taken, first in sources:
+        for k in taken:
+            tile = chosen_ref[a, k]
+            chunk = lax.div(tile, per)
+            place = places[0]
+            for other in range(1, n_place):
+                place = jnp.where(chunk == other, places[other], place)
+            s = (i * n_place + place) * per + lax.rem(tile, per)
+            at = count_ref[s]
+            entry_ref[s * n_held + at] = first + k - taken[0]
+            count_ref[s] = at + 1
+
+
+def tile_copy(tiles_ref, held_ref, came, a, k, i, e):
+    return pltpu.make_async_copy(tiles_ref.at[a, k], held_ref.at[i, e], came.at[i, e])
+
+
+def add_up(s, i, held_ref, count_ref, entry_ref, into_ref, first_ref=None):
+    n_entry, width = held_ref.shape[1], held_ref.shape[2]
+    named = count_ref[s]
+
+    def tile(m, rows):
+        return held_ref[i, entry_ref[s * n_entry + m], rows, :]
+
+    for exact in range(MOST + 1):
+        @pl.when(named == exact)
+        def _():
+            @pl.loop(0, width // STEP)
+            def _(r):
+                rows = pl.ds(pl.multiple_of(r * STEP, STEP), STEP)
+                parts = [] if first_ref is None else [first_ref[rows, :]]
+                parts += [tile(m, rows) for m in range(exact)]
+                if not parts:
+                    total = jnp.zeros((STEP, width), into_ref.dtype)
+                elif len(parts) == 2:
+                    total = parts[0] + parts[1]
+                else:
+                    total = parts[0]
+                    for part in parts[1:]:
+                        total = total.astype(jnp.float32) + part.astype(jnp.float32)
+                into_ref[rows, :] = total.astype(into_ref.dtype)
+
+    @pl.when(named > MOST)
+    def _():
+        @pl.loop(0, width // STEP)
+        def _(r):
+            rows = pl.ds(pl.multiple_of(r * STEP, STEP), STEP)
+
+            def add(m, total):
+                return total + tile(m, rows).astype(jnp.float32)
+
+            total = tile(0, rows) if first_ref is None else first_ref[rows, :]
+            first = 1 if first_ref is None else 0
+            total = lax.fori_loop(first, named, add, total.astype(jnp.float32))
+            into_ref[rows, :] = total.astype(into_ref.dtype)
+
+
+def add_product(s, i, held_ref, count_ref, entry_ref, sums_ref, amps_ref, total_ref):
+    n_entry = held_ref.shape[1]
+    named = count_ref[s]
+
+    def multiply(block):
+        total_ref[...] += jnp.dot(amps_ref[...], block, preferred_element_type=jnp.float32)
+
+    for exact in range(1, MOST + 1):
+        @pl.when(named == exact)
+        def _():
+            tiles = [held_ref[i, entry_ref[s * n_entry + m]] for m in range(exact)]
+            block = tiles[0]
+            if exact == 2:
+                block = tiles[0] + tiles[1]
+            elif exact > 2:
+                block = sum(tile.astype(jnp.float32) for tile in tiles).astype(jnp.bfloat16)
+            multiply(block)
+
+    @pl.when(named > MOST)
+    def _():
+        add_up(s, i, held_ref, count_ref, entry_ref, sums_ref)
+        multiply(sums_ref[...])
+
+
+def sums_kernel(vir_ref, chosen_ref, other_ref, tiles_ref, *refs, a, taken, extra):
+    sums_ref, there_ref, list_count, list_entry, held_ref, came, count_ref, entry_ref = refs[-8:]
+    n_place, per = sums_ref.shape[:2]
+    n_own, n_entry = chosen_ref.shape
+    n_held = held_ref.shape[1]
+    list_entries(vir_ref[0], [(chosen_ref, a, 0, taken, 0)], count_ref, entry_ref, per, n_held)
+
+    @pl.loop(0, n_place * per)
+    def _(s):
+        @pl.loop(0, count_ref[s])
+        def _(m):
+            e = entry_ref[s * n_held + m]
+            tile_copy(tiles_ref, held_ref, came, a, e + taken[0], 0, e).start()
+
+    there_ref[...] = jnp.zeros_like(there_ref)
+    if extra is not None:
+        sources = [(other_ref, b, b, range(n_entry), 0) for b in range(n_own)]
+        sources += [(chosen_ref, 0, 0, extra, n_entry)] * (len(extra) > 0)
+        list_entries(vir_ref[0], sources, list_count, list_entry, per, n_entry + len(extra))
+
+    @pl.loop(0, n_place * per)
+    def _(s):
+        @pl.loop(0, count_ref[s])
+        def _(m):
+            e = entry_ref[s * n_held + m]
+            tile_copy(tiles_ref, held_ref, came, a, 0, 0, e).wait()
+
+        add_up(s, 0, held_ref, count_ref, entry_ref, sums_ref.at[lax.div(s, per), lax.rem(s, per)])
+
+
+def tile_sums(vir, chosen, other, tiles, a, taken, extra, per, first):
+    n_own, n_entry, width, _ = tiles.shape
+    n_place = len(ARRIVAL[0])
+    n_tile = n_place * per
+    n_list, n_held = (1, 8) if extra is None else (n_own * n_tile, n_entry + len(extra))
+    smem, vmem = pl.BlockSpec(memory_space=pltpu.SMEM), pl.BlockSpec(memory_space=pltpu.VMEM)
+    return pl.pallas_call(
+        functools.partial(sums_kernel, a=a, taken=taken, extra=extra),
+        in_specs=[smem] * 3 + [pl.BlockSpec(memory_space=pl.ANY)] * (1 + len(first)),
+        out_specs=[vmem] * 2 + [smem] * 2,
+        out_shape=[
+            jax.ShapeDtypeStruct((n_place, per, width, width), jnp.bfloat16),
+            jax.ShapeDtypeStruct((16, 128), jnp.bfloat16),
+            jax.ShapeDtypeStruct((n_list,), jnp.int32),
+            jax.ShapeDtypeStruct((n_list * n_held,), jnp.int32),
+        ],
+        scratch_shapes=[
+            pltpu.VMEM((1, len(taken), width, width), jnp.bfloat16),
+            pltpu.SemaphoreType.DMA((1, len(taken))),
+            pltpu.SMEM((n_tile,), jnp.int32),
+            pltpu.SMEM((n_tile * len(taken),), jnp.int32),
+        ],
+        compiler_params=pltpu.CompilerParams(vmem_limit_bytes=44 * MIB),
+        cost_estimate=pl.CostEstimate(flops=0, bytes_accessed=1000000, transcendentals=0),
+    )(vir, chosen, other, tiles, *first)
+
+
+def early_kernel(vir_ref, rep_ref, count_ref, entry_ref, occ_ref, pair_ref, mine0_ref, mine1_ref, *refs, extra):
+    other_ref, own_ref, refs = refs[0], refs[1], refs[2:]
+    pieces, refs = refs[:4 * PIECES], refs[4 * PIECES:]
+    total_ref, last_ref, inner_ref, held_ref, came, sums_ref, amps_ref = refs
+    mine_refs = (mine0_ref, mine1_ref)
+    vir_index = vir_ref[0]
+    inner = (vir_index == 1) | (vir_index == 2)
+    inner_ref[...] = jnp.full(inner_ref.shape, jnp.where(inner, 1.0, 0.0), jnp.float32)
+    n_own, n_held, width, _ = held_ref.shape
+    n_entry = n_held - len(extra)
+    n_place, per = mine0_ref.shape[:2]
+
+    def slot_of(place, a, t):
+        return (a * n_place + place) * per + t
+
+    def start_copies(place):
+        for a in range(n_own):
+            @pl.loop(0, per)
+            def _(t):
+                s = slot_of(place, a, t)
+
+                @pl.loop(0, count_ref[s])
+                def _(m):
+                    e = entry_ref[s * n_held + m]
+
+                    @pl.when(e < n_entry)
+                    def _():
+                        tile_copy(other_ref, held_ref, came, a, e, a, e).start()
+
+                    if len(extra) and a == 0:
+                        @pl.when(e >= n_entry)
+                        def _():
+                            tile_copy(own_ref, held_ref, came, a, e - n_entry + extra[0], a, e).start()
+
+    def wait_copies(s, a):
+        @pl.loop(0, count_ref[s])
+        def _(m):
+            e = entry_ref[s * n_held + m]
+            tile_copy(other_ref, held_ref, came, a, 0, a, e).wait()
+
+    start_copies(n_place - 1)
+    pl.loop(0, n_place - 1)(start_copies)
+
+    all_rows, wide = amps_ref.shape[0], per * width
+    rows = all_rows // PIECES
+    for i in range(PIECES):
+        own, near, mid, mid_out = pieces[i::PIECES]
+        part = slice(i * rows, (i + 1) * rows)
+        amps_ref[part, :wide] = own[...]
+        amps_ref[part, wide:2 * wide] = near[...]
+        amps_ref[part, 2 * wide:] = jnp.where(inner, mid[...], mid_out[...])
+    own_occ = occ_ref[:, :all_rows]
+    for rep in range(1, occ_ref.shape[1] // all_rows):
+        own_occ = jnp.where(rep_ref[0] == rep, occ_ref[:, rep * all_rows:(rep + 1) * all_rows], own_occ)
+    down = jnp.broadcast_to(own_occ, (128, all_rows)).T
+    down = jnp.concatenate([down] * (width // 128), axis=1)
+    for a in range(n_own):
+        columns = slice(a * width, (a + 1) * width)
+        gap = pair_ref[:, columns] - down
+        total_ref[a] = gap * amps_ref[:, columns].astype(jnp.float32) + jnp.dot(
+            amps_ref[...], mine_refs[a][:n_place - 1].reshape(-1, width), preferred_element_type=jnp.float32
+        )
+
+    for a in range(n_own):
+        @pl.loop(0, per)
+        def _(t):
+            s = slot_of(n_place - 1, a, t)
+            wait_copies(s, a)
+            add_up(s, a, held_ref, count_ref, entry_ref, last_ref.at[a, t], mine_refs[a].at[n_place - 1, t])
+
+    @pl.loop(0, n_place - 1)
+    def _(place):
+        for a in range(n_own):
+            @pl.loop(0, per)
+            def _(t):
+                s = slot_of(place, a, t)
+                columns = pl.ds(pl.multiple_of((place * per + t) * width, width), width)
+                wait_copies(s, a)
+                add_product(
+                    s, a, held_ref, count_ref, entry_ref, sums_ref, amps_ref.at[:, columns], total_ref.at[a]
+                )
+
+
+def early_products(vir, rep, count, entry, occ, pair, mine, other, tiles, extra, own, near, mid, mid_out):
+    rows, columns = own[0].shape[0] * PIECES, own[0].shape[1]
+    n_own, n_entry, width, _ = tiles.shape
+    n_place, per = len(ARRIVAL[0]), columns // width
+    smem, vmem = pl.BlockSpec(memory_space=pltpu.SMEM), pl.BlockSpec(memory_space=pltpu.VMEM)
+    return pl.pallas_call(
+        functools.partial(early_kernel, extra=extra),
+        in_specs=[smem] * 4 + [vmem] * 4 + [pl.BlockSpec(memory_space=pl.ANY)] * 2 + [vmem] * (4 * PIECES),
+        out_specs=[vmem] * 3,
+        out_shape=[
+            jax.ShapeDtypeStruct((n_own, rows, width), jnp.float32),
+            jax.ShapeDtypeStruct((n_own, per, width, width), jnp.bfloat16),
+            jax.ShapeDtypeStruct((8, 128), jnp.float32),
+        ],
+        scratch_shapes=[
+            pltpu.VMEM((n_own, n_entry + len(extra), width, width), jnp.bfloat16),
+            pltpu.SemaphoreType.DMA((n_own, n_entry + len(extra))),
+            pltpu.VMEM((width, width), jnp.bfloat16),
+            pltpu.VMEM((rows, (n_place - 1) * columns), jnp.bfloat16),
+        ],
+        compiler_params=pltpu.CompilerParams(vmem_limit_bytes=34 * MIB),
+        cost_estimate=pl.CostEstimate(
+            flops=2 * n_place * rows * columns * columns, bytes_accessed=2 * tiles.size, transcendentals=0
+        ),
+    )(vir, rep, count, entry, occ, pair, *mine, other, tiles, *own, *near, *mid, *mid_out)
+
+
+def there_kernel(*refs):
+    refs[-1][...] = jnp.zeros_like(refs[-1])
+
+
+def all_there(*arrays):
+    return pl.pallas_call(
+        there_kernel,
+        in_specs=[pl.BlockSpec(memory_space=pl.ANY)] * len(arrays),
+        out_specs=pl.BlockSpec(memory_space=pltpu.VMEM),
+        out_shape=jax.ShapeDtypeStruct((16, 128), jnp.bfloat16),
+        compiler_params=pltpu.CompilerParams(vmem_limit_bytes=MIB),
+        cost_estimate=pl.CostEstimate(flops=0, bytes_accessed=1000000, transcendentals=0),
+    )(*arrays)
+
+
+def last_kernel(total_ref, sums_ref, inner_ref, *refs, piece):
+    far, far_out_ref, (resid_ref, rows_ref, gone) = refs[:PIECES], refs[PIECES], refs[-3:]
+    n_own, _, width, _ = sums_ref.shape
+    rows = far_out_ref.shape[0]
+
+    def finish(piece, amps_ref):
+        part, held = pl.ds(piece * rows, rows), rows_ref.at[piece]
+        for a in range(n_own):
+            columns = pl.ds(a * width, width)
+            product = jnp.dot(amps_ref[...], sums_ref[a].reshape(-1, width), preferred_element_type=jnp.float32)
+            held[:, columns] = (total_ref[a, part] + product).astype(rows_ref.dtype)
+            pltpu.make_async_copy(held.at[:, columns], resid_ref.at[part, columns], gone.at[piece, a]).start()
+
+    def wait(piece):
+        part, held = pl.ds(piece * rows, rows), rows_ref.at[piece]
+        for a in range(n_own):
+            columns = pl.ds(a * width, width)
+            pltpu.make_async_copy(held.at[:, columns], resid_ref.at[part, columns], gone.at[piece, a]).wait()
+
+    inner = inner_ref[0, 0] > 0
+
+    @pl.when(jnp.logical_not(inner))
+    def _():
+        finish(piece, far_out_ref)
+        wait(piece)
+
+    if piece == 0:
+        @pl.when(inner)
+        def _():
+            for i in range(PIECES):
+                finish(i, far[i])
+            for i in range(PIECES):
+                wait(i)
+
+
+def last_product(total, sums, inner, far, far_out, piece, resid=None, there=()):
+    n_own, rows, width = total.shape
+    vmem, anywhere = pl.BlockSpec(memory_space=pltpu.VMEM), pl.BlockSpec(memory_space=pl.ANY)
+    others = [*there] if resid is None else [resid, *there]
+    shape = (rows, n_own * width)
+    return pl.pallas_call(
+        functools.partial(last_kernel, piece=piece),
+        in_specs=[vmem] * (4 + PIECES) + [anywhere] * len(others),
+        out_specs=anywhere,
+        out_shape=jax.ShapeDtypeStruct(shape, jnp.bfloat16),
+        input_output_aliases={} if resid is None else {4 + PIECES: 0},
+        scratch_shapes=[
+            pltpu.VMEM((PIECES, rows // PIECES, shape[1]), jnp.bfloat16),
+            pltpu.SemaphoreType.DMA((PIECES, n_own)),
+        ],
+        compiler_params=pltpu.CompilerParams(vmem_limit_bytes=16 * MIB),
+        cost_estimate=pl.CostEstimate(flops=0, bytes_accessed=1000000, transcendentals=0),
+    )(total, sums, inner, *far, far_out, *others)
+
+
+def dense_local(amplitudes, integrals, cd_tiles, occ_energy, pair_energy):
+    rows = amplitudes.shape[0] // lax.axis_size("rep")
+    rep_index, vir_index = lax.axis_index("rep"), lax.axis_index("vir")
+    swap_near, swap_mid, outward = [(0, 1), (1, 0), (2, 3), (3, 2)], [(1, 2), (2, 1)], [(1, 0), (2, 3)]
+    swap_rep = [(0, 1), (1, 0)]
+
+    def send(pieces, pairs):
+        return [lax.ppermute(piece, "vir", pairs) for piece in pieces]
+
+    piece = rows // PIECES
+    own = [
+        lax.dynamic_slice_in_dim(amplitudes, rep_index * rows + i * piece, piece, 0) for i in range(PIECES)
+    ]
+    vir, rep = vir_index.reshape(1), rep_index.reshape(1)
+    occ, pair = occ_energy[None, :], pair_energy[None, :]
+    per = amplitudes.shape[1] // integrals.shape[2]
+    marks = []
+
+    def after(mark, *held):
+        *held, mark = lax.optimization_barrier((*held, mark))
+        marks.append(mark)
+        return held
+
+    other = lax.ppermute(integrals, "rep", swap_rep)
+    chosen_other = lax.ppermute(cd_tiles, "rep", swap_rep)
+    near, mid = send(own, swap_near), send(own, swap_mid)
+    n_entry = integrals.shape[1]
+    taken, extra = range(n_entry * 8 // 12), range(n_entry * 8 // 12, n_entry)
+    mine0, mark, _, _ = tile_sums(vir, cd_tiles, cd_tiles, integrals, 0, taken, None, per, (near[0], mid[0]))
+    near[1], mid[1] = after(mark, near[1], mid[1])
+    far, mid_out = send(near, swap_mid), send(mid, outward)
+    far[0], mid_out[0] = after(all_there(near[1], mid[1]), far[0], mid_out[0])
+    mine1, mark, count, entry = tile_sums(
+        vir, cd_tiles, chosen_other, integrals, 1, range(n_entry), extra, per, (far[0], mid_out[0])
+    )
+    mid_out[1], = after(mark, mid_out[1])
+    far[1], = after(all_there(mid_out[1]), far[1])
+    far_out = send(far, outward)
+    total, sums, inner = early_products(
+        vir, rep, count, entry, occ, pair, (mine0, mine1), other, integrals, extra, own, near, mid, mid_out
+    )
+    resid = last_product(total, sums, inner, far, far_out[0], 0, there=marks)
+    return last_product(total, sums, inner, far, far_out[1], 1, resid)
+
+
 def solution(mesh):
     in_specs = (P("occ", "vir"), P("vir", "rep", None, None), P("vir", "rep"), P("occ"), P("vir"))
     out_specs = P(("occ", "rep"), "vir")
+    n_rep = mesh.shape["rep"]
+
+    def local(amplitudes, integrals, cd_tiles, occ_energy, pair_energy):
+        n_tile = amplitudes.shape[1] * mesh.shape["vir"] // integrals.shape[2]
+        few_tiles = n_tile <= n_rep * integrals.shape[1]
+        few_tiles &= n_rep == 2 and mesh.shape["vir"] == 4 and integrals.shape[0] == 2 and integrals.shape[1] % 3 == 0
+        body = dense_local if few_tiles else sparse_local
+        return body(amplitudes, integrals, cd_tiles, occ_energy, pair_energy)
+
     return jax.shard_map(local, mesh=mesh, in_specs=in_specs, out_specs=out_specs, check_vma=False)

time: 137 us -> 43.5 us (0.32)
  the two profiles are of different devices: /device:TPU:18 before, /device:TPU:17 now
where the time goes in v1:
time: 43.5 us; the launch traced here: 43 us
  Pallas kernels  18.6 us (43%)
  starting transfers between devices  18.4 us (42%)
  waiting for transfers between devices  3.96 us (9%)
  local copies, waits for them, and re-layouts  1.75 us (4%)
    ppermute x10, starting transfers between devices, send(): return [lax.ppermute(piece, 'vir', pairs) for piece in pieces]  16.3 us
    pallas_call x1, Pallas kernels, early_products(): pl.pallas_call(functools.partial(early_kernel, extra=extra), in_specs=[sm...  9.01 us
    pallas_call x2, Pallas kernels, tile_sums(): pl.pallas_call(functools.partial(sums_kernel, a=a, taken=taken, extra=ext...  7.99 us
    ppermute x10, waiting for transfers between devices, send(): return [lax.ppermute(piece, 'vir', pairs) for piece in pieces]  3.95 us
    pallas_call x2, Pallas kernels, last_product(): pl.pallas_call(functools.partial(last_kernel, piece=piece), in_specs=[vme...  1.6 us
    ppermute x1, starting transfers between devices, dense_local(): chosen_other = lax.ppermute(cd_tiles, 'rep', swap_rep)  1.41 us
    dynamic_slice x1, local copies, waits for them, and re-layouts, dense_local(): lax.dynamic_slice_in_dim(amplitudes, rep_index * rows + i * piece, piece, 0)  1.06 us
  transfers between devices with their start and end apart: 12, of which 3 were waited for; matrix products, arithmetic and copies ran while one was open for 2% of the time, Pallas kernels for 43%

profile of v1, /device:TPU:17, one launch (start us, length us, event | category | flops | bytes accessed | tf_op | source)
XLA Modules:
  0.0 43.0 jit_solution(12095918539187489526)
XLA Ops:
  0.0 0.7 %collective-permute-start.7 = (bf16[2,12,512,512]{3,2,1,0:T(8,128)(2,1)}, bf16[2,12,512,512]{3,2,1,0:T(8,128)(2,1)}, u32[]{:S(2)}, u32[]{:S(2)}) collective-permute-start(bf16[2,12,512,512]{3,2,1,0:T(8,128)(2,1)} %refs_1_.1), channel_id=1, source_target_pairs={{0,1},{1,0},{2,3},{3,2},{4,5},{5,4},{6,7},{7,6},{8,9},{9,8},{10,11... | collective-permute-start | bytes 37748744 | tf_op jit(solution)/shard_map/ppermute | solution.py:403
  0.7 1.1 %constant_dynamic-slice_fusion = (bf16[128,1024]{1,0:T(8,128)(2,1)S(1)}, bf16[128,1024]{1,0:T(8,128)(2,1)S(1)}) fusion(bf16[512,1024]{1,0:T(8,128)(2,1)} %param.5, s32[]{:T(128)S(6)} %select_n.7, s32[]{:T(128)S(6)} %select_n.6), kind=kLoop, calls=%fused_computation | loop fusion | bytes 1048584 | tf_op jit(solution)/shard_map/dynamic_slice | solution.py:391
  1.7 1.4 %collective-permute-start.1 = (bf16[128,1024]{1,0:T(8,128)(2,1)S(1)}, bf16[128,1024]{1,0:T(8,128)(2,1)S(1)}, u32[]{:S(2)}, u32[]{:S(2)}) collective-permute-start(bf16[128,1024]{1,0:T(8,128)(2,1)S(1)} %get-tuple-element.44.refs_2_), channel_id=1, source_target_pairs={{0,2},{2,0},{4,6},{6,4},{1,3},{3,1},{5,7},{7,5},{8,10},{10,8},{12,... | collective-permute-start | bytes 786440 | tf_op jit(solution)/shard_map/ppermute | solution.py:387
  3.1 1.9 %collective-permute-start.3 = (bf16[128,1024]{1,0:T(8,128)(2,1)S(1)}, bf16[128,1024]{1,0:T(8,128)(2,1)S(1)}, u32[]{:S(2)}, u32[]{:S(2)}) collective-permute-start(bf16[128,1024]{1,0:T(8,128)(2,1)S(1)} %get-tuple-element.44.refs_2_), channel_id=1, source_target_pairs={{2,4},{4,2},{3,5},{5,3},{10,12},{12,10},{11,13},{13,11},{18,20},{2... | collective-permute-start | bytes 786440 | tf_op jit(solution)/shard_map/ppermute | solution.py:387
  5.0 0.1 collective-permute-start.5
  5.1 3.4 %collective-permute-start.6 = (bf16[128,1024]{1,0:T(8,128)(2,1)S(1)}, bf16[128,1024]{1,0:T(8,128)(2,1)S(1)}, u32[]{:S(2)}, u32[]{:S(2)}) collective-permute-start(bf16[128,1024]{1,0:T(8,128)(2,1)S(1)} %get-tuple-element.43.refs_3_), channel_id=1, source_target_pairs={{2,4},{4,2},{3,5},{5,3},{10,12},{12,10},{11,13},{13,11},{18,20},{2... | collective-permute-start | bytes 786440 | tf_op jit(solution)/shard_map/ppermute | solution.py:387
  8.5 1.3 %collective-permute-done.1.refs_0_.refs_4_ = bf16[128,1024]{1,0:T(8,128)(2,1)S(1)} collective-permute-done((bf16[128,1024]{1,0:T(8,128)(2,1)S(1)}, bf16[128,1024]{1,0:T(8,128)(2,1)S(1)}, u32[]{:S(2)}, u32[]{:S(2)}) %collective-permute-start.1) | collective-permute-done | bytes 262176 | tf_op jit(solution)/shard_map/ppermute | solution.py:387
  9.7 2.1 %collective-permute-start.2 = (bf16[128,1024]{1,0:T(8,128)(2,1)S(1)}, bf16[128,1024]{1,0:T(8,128)(2,1)S(1)}, u32[]{:S(2)}, u32[]{:S(2)}) collective-permute-start(bf16[128,1024]{1,0:T(8,128)(2,1)S(1)} %collective-permute-done.1.refs_0_.refs_4_), channel_id=1, source_target_pairs={{2,4},{4,2},{3,5},{5,3},{10,12},{12,10},{11,13},{13,11},{18,20},{2... | collective-permute-start | bytes 786440 | tf_op jit(solution)/shard_map/ppermute | solution.py:387
  11.8 0.8 %collective-permute-done.3.refs_1_.refs_6_ = bf16[128,1024]{1,0:T(8,128)(2,1)S(1)} collective-permute-done((bf16[128,1024]{1,0:T(8,128)(2,1)S(1)}, bf16[128,1024]{1,0:T(8,128)(2,1)S(1)}, u32[]{:S(2)}, u32[]{:S(2)}) %collective-permute-start.3) | collective-permute-done | bytes 262176 | tf_op jit(solution)/shard_map/ppermute | solution.py:387
  12.6 1.3 %collective-permute-start.4 = (bf16[128,1024]{1,0:T(8,128)(2,1)S(1)}, bf16[128,1024]{1,0:T(8,128)(2,1)S(1)}, u32[]{:S(2)}, u32[]{:S(2)}) collective-permute-start(bf16[128,1024]{1,0:T(8,128)(2,1)S(1)} %collective-permute-done.3.refs_1_.refs_6_), channel_id=1, source_target_pairs={{2,0},{4,6},{3,1},{5,7},{10,8},{12,14},{11,9},{13,15},{18,16},{20,... | collective-permute-start | bytes 786440 | tf_op jit(solution)/shard_map/ppermute | solution.py:387
  13.9 0.0 copy-start
  13.9 0.7 %copy-done = s32[2,12]{1,0:T(2,128)S(1)} copy-done((s32[2,12]{1,0:T(2,128)S(1)}, s32[2,12]{1,0:T(2,128)}, u32[]{:S(2)}) %copy-start) | copy-done | bytes 120
  14.6 3.6 %shard_map.55 = (bf16[4,2,512,512]{3,2,1,0:T(8,128)(2,1)S(1)}, bf16[16,128]{1,0:T(8,128)(2,1)S(1)}, s32[1]{0:T(128)}, s32[8]{0:T(128)}) custom-call(s32[1]{0:T(128)} %bitcast.vir_ref, s32[2,12]{1,0:T(2,128)S(1)} %copy-done, s32[2,12]{1,0:T(2,128)S(1)} %copy-done, bf16[2,12,512,512]{3,2,1,0:T(8,128)(2,1)} %refs_1_.1, ...), custom_call_target="tpu_custom_call" | custom-call | bytes 1000000 | tf_op jit(solution)/shard_map/pallas_call | solution.py:179
  18.2 0.0 collective-permute-done.5.refs_0_.refs_5_
  18.2 0.0 collective-permute-done.6.refs_1_.refs_7_
  18.2 1.3 %collective-permute-start.8 = (bf16[128,1024]{1,0:T(8,128)(2,1)S(1)}, bf16[128,1024]{1,0:T(8,128)(2,1)S(1)}, u32[]{:S(2)}, u32[]{:S(2)}) collective-permute-start(bf16[128,1024]{1,0:T(8,128)(2,1)S(1)} %collective-permute-done.6.refs_1_.refs_7_), channel_id=1, source_target_pairs={{2,0},{4,6},{3,1},{5,7},{10,8},{12,14},{11,9},{13,15},{18,16},{20,... | collective-permute-start | bytes 786440 | tf_op jit(solution)/shard_map/ppermute | solution.py:387
  19.6 2.4 %collective-permute-start.9 = (bf16[128,1024]{1,0:T(8,128)(2,1)S(1)}, bf16[128,1024]{1,0:T(8,128)(2,1)S(1)}, u32[]{:S(2)}, u32[]{:S(2)}) collective-permute-start(bf16[128,1024]{1,0:T(8,128)(2,1)S(1)} %collective-permute-done.5.refs_0_.refs_5_), channel_id=1, source_target_pairs={{2,4},{4,2},{3,5},{5,3},{10,12},{12,10},{11,13},{13,11},{18,20},{2... | collective-permute-start | bytes 786440 | tf_op jit(solution)/shard_map/ppermute | solution.py:387
  21.9 0.0 copy-start.2
  22.0 0.0 copy-start.3
  22.0 1.9 %collective-permute-done.2.refs_0_ = bf16[128,1024]{1,0:T(8,128)(2,1)S(1)} collective-permute-done((bf16[128,1024]{1,0:T(8,128)(2,1)S(1)}, bf16[128,1024]{1,0:T(8,128)(2,1)S(1)}, u32[]{:S(2)}, u32[]{:S(2)}) %collective-permute-start.2) | collective-permute-done | bytes 262176 | tf_op jit(solution)/shard_map/ppermute | solution.py:387
  23.8 1.4 %collective-permute-start = (s32[2,12]{1,0:T(2,128)S(1)}, s32[2,12]{1,0:T(2,128)S(1)}, u32[]{:S(2)}, u32[]{:S(2)}) collective-permute-start(s32[2,12]{1,0:T(2,128)S(1)} %copy-done), channel_id=1, source_target_pairs={{0,1},{1,0},{2,3},{3,2},{4,5},{5,4},{6,7},{7,6},{8,9},{9,8},{10,11... | collective-permute-start | bytes 296 | tf_op jit(solution)/shard_map/ppermute | solution.py:404
  25.3 0.0 collective-permute-done.4.refs_1_.refs_8_
  25.3 1.3 %collective-permute-start.11 = (bf16[128,1024]{1,0:T(8,128)(2,1)S(1)}, bf16[128,1024]{1,0:T(8,128)(2,1)S(1)}, u32[]{:S(2)}, u32[]{:S(2)}) collective-permute-start(bf16[128,1024]{1,0:T(8,128)(2,1)S(1)} %collective-permute-done.2.refs_0_), channel_id=1, source_target_pairs={{2,0},{4,6},{3,1},{5,7},{10,8},{12,14},{11,9},{13,15},{18,16},{20,... | collective-permute-start | bytes 786440 | tf_op jit(solution)/shard_map/ppermute | solution.py:387
  26.6 0.0 collective-permute-done.other_ref
  26.6 4.4 %shard_map.57 = (bf16[4,2,512,512]{3,2,1,0:T(8,128)(2,1)S(1)}, bf16[16,128]{1,0:T(8,128)(2,1)S(1)}, s32[16]{0:T(128)S(1)}, s32[256]{0:T(256)S(1)}) custom-call(s32[1]{0:T(128)} %bitcast.vir_ref, s32[2,12]{1,0:T(2,128)S(1)} %copy-done.1, s32[2,12]{1,0:T(2,128)S(1)} %collective-permute-done.other_ref, bf16[2,12,512,512]{3,2,1,0:T(8,128)(2,1)} %refs_1_.1, ...), custom_call_target="tpu_custom_call" | custom-call | bytes 1000000 | tf_op jit(solution)/shard_map/pallas_call | solution.py:179
  30.9 0.0 collective-permute-done.8.refs_9_.refs_0_
  31.0 0.0 collective-permute-done.9.refs_1_
  31.0 1.3 %collective-permute-start.10 = (bf16[128,1024]{1,0:T(8,128)(2,1)S(1)}, bf16[128,1024]{1,0:T(8,128)(2,1)S(1)}, u32[]{:S(2)}, u32[]{:S(2)}) collective-permute-start(bf16[128,1024]{1,0:T(8,128)(2,1)S(1)} %collective-permute-done.9.refs_1_), channel_id=1, source_target_pairs={{2,0},{4,6},{3,1},{5,7},{10,8},{12,14},{11,9},{13,15},{18,16},{20,... | collective-permute-start | bytes 786440 | tf_op jit(solution)/shard_map/ppermute | solution.py:387
  32.3 9.0 %shard_map.58 = (f32[2,256,512]{2,1,0:T(8,128)S(1)}, bf16[2,2,512,512]{3,2,1,0:T(8,128)(2,1)S(1)}, f32[8,128]{1,0:T(8,128)S(1)}) custom-call(s32[1]{0:T(128)} %bitcast.vir_ref, s32[1]{0:T(128)} %bitcast.1.rep_ref, s32[16]{0:T(128)S(1)} %get-tuple-element.29.count_ref, s32[256]{0:T(256)S(1)} %get-tuple-element.30.entry_ref, f32[1,512]{1,0:T(1,128)S(1)} %bitcast.5, ...), custom_call_target="tpu_custom_call" | custom-call | flops 2147483648 | bytes 12582912 | tf_op jit(solution)/shard_map/pallas_call | solution.py:288
  41.3 0.0 collective-permute-done.11.refs_2_
  41.3 1.5 %shard_map.60.refs_3_ = bf16[256,1024]{1,0:T(8,128)(2,1)} custom-call(f32[2,256,512]{2,1,0:T(8,128)S(1)} %get-tuple-element.35.total_ref, bf16[2,2,512,512]{3,2,1,0:T(8,128)(2,1)S(1)} %get-tuple-element.36.sums_ref, f32[8,128]{1,0:T(8,128)S(1)} %get-tuple-element.37.inner_ref, bf16[128,1024]{1,0:T(8,128)(2,1)S(1)} %collective-permute-done.2.refs_0_, ...), custom_call_target="tpu_custom_call" | custom-call | bytes 1000000 | tf_op jit(solution)/shard_map/pallas_call | solution.py:365
  42.9 0.1 shard_map.61
  (8 shorter events, 0.0 us)
Async XLA Ops:
  0.0 32.3 %collective-permute-start.7 = (bf16[2,12,512,512]{3,2,1,0:T(8,128)(2,1)}, bf16[2,12,512,512]{3,2,1,0:T(8,128)(2,1)}, u32[]{:S(2)}, u32[]{:S(2)}) collective-permute-start(bf16[2,12,512,512]{3,2,1,0:T(8,128)(2,1)} %refs_1_.1), channel_id=1, source_target_pairs={{0,1},{1,0},{2,3},{3,2},{4,5},{5,4},{6,7},{7,6},{8,9},{9,8},{10,11... | collective-permute-start | bytes 37748744 | tf_op jit(solution)/shard_map/ppermute | solution.py:403
  1.7 8.0 %collective-permute-start.1 = (bf16[128,1024]{1,0:T(8,128)(2,1)S(1)}, bf16[128,1024]{1,0:T(8,128)(2,1)S(1)}, u32[]{:S(2)}, u32[]{:S(2)}) collective-permute-start(bf16[128,1024]{1,0:T(8,128)(2,1)S(1)} %get-tuple-element.44.refs_2_), channel_id=1, source_target_pairs={{0,2},{2,0},{4,6},{6,4},{1,3},{3,1},{5,7},{7,5},{8,10},{10,8},{12,... | collective-permute-start | bytes 786440 | tf_op jit(solution)/shard_map/ppermute | solution.py:387
  3.1 9.5 %collective-permute-start.3 = (bf16[128,1024]{1,0:T(8,128)(2,1)S(1)}, bf16[128,1024]{1,0:T(8,128)(2,1)S(1)}, u32[]{:S(2)}, u32[]{:S(2)}) collective-permute-start(bf16[128,1024]{1,0:T(8,128)(2,1)S(1)} %get-tuple-element.44.refs_2_), channel_id=1, source_target_pairs={{2,4},{4,2},{3,5},{5,3},{10,12},{12,10},{11,13},{13,11},{18,20},{2... | collective-permute-start | bytes 786440 | tf_op jit(solution)/shard_map/ppermute | solution.py:387
  5.0 13.2 %collective-permute-start.5 = (bf16[128,1024]{1,0:T(8,128)(2,1)S(1)}, bf16[128,1024]{1,0:T(8,128)(2,1)S(1)}, u32[]{:S(2)}, u32[]{:S(2)}) collective-permute-start(bf16[128,1024]{1,0:T(8,128)(2,1)S(1)} %get-tuple-element.43.refs_3_), channel_id=1, source_target_pairs={{0,2},{2,0},{4,6},{6,4},{1,3},{3,1},{5,7},{7,5},{8,10},{10,8},{12,... | collective-permute-start | bytes 786440 | tf_op jit(solution)/shard_map/ppermute | solution.py:387
  5.1 13.1 %collective-permute-start.6 = (bf16[128,1024]{1,0:T(8,128)(2,1)S(1)}, bf16[128,1024]{1,0:T(8,128)(2,1)S(1)}, u32[]{:S(2)}, u32[]{:S(2)}) collective-permute-start(bf16[128,1024]{1,0:T(8,128)(2,1)S(1)} %get-tuple-element.43.refs_3_), channel_id=1, source_target_pairs={{2,4},{4,2},{3,5},{5,3},{10,12},{12,10},{11,13},{13,11},{18,20},{2... | collective-permute-start | bytes 786440 | tf_op jit(solution)/shard_map/ppermute | solution.py:387
  9.7 14.1 %collective-permute-start.2 = (bf16[128,1024]{1,0:T(8,128)(2,1)S(1)}, bf16[128,1024]{1,0:T(8,128)(2,1)S(1)}, u32[]{:S(2)}, u32[]{:S(2)}) collective-permute-start(bf16[128,1024]{1,0:T(8,128)(2,1)S(1)} %collective-permute-done.1.refs_0_.refs_4_), channel_id=1, source_target_pairs={{2,4},{4,2},{3,5},{5,3},{10,12},{12,10},{11,13},{13,11},{18,20},{2... | collective-permute-start | bytes 786440 | tf_op jit(solution)/shard_map/ppermute | solution.py:387
  12.6 12.7 %collective-permute-start.4 = (bf16[128,1024]{1,0:T(8,128)(2,1)S(1)}, bf16[128,1024]{1,0:T(8,128)(2,1)S(1)}, u32[]{:S(2)}, u32[]{:S(2)}) collective-permute-start(bf16[128,1024]{1,0:T(8,128)(2,1)S(1)} %collective-permute-done.3.refs_1_.refs_6_), channel_id=1, source_target_pairs={{2,0},{4,6},{3,1},{5,7},{10,8},{12,14},{11,9},{13,15},{18,16},{20,... | collective-permute-start | bytes 786440 | tf_op jit(solution)/shard_map/ppermute | solution.py:387
  13.9 0.7 %copy-start = (s32[2,12]{1,0:T(2,128)S(1)}, s32[2,12]{1,0:T(2,128)}, u32[]{:S(2)}) copy-start(s32[2,12]{1,0:T(2,128)} %chosen_ref.3) | copy-start | bytes 292
  14.6 12.0 %copy-start.1 = (s32[2,12]{1,0:T(2,128)S(1)}, s32[2,12]{1,0:T(2,128)}, u32[]{:S(2)}) copy-start(s32[2,12]{1,0:T(2,128)} %chosen_ref.3) | copy-start | bytes 292
  18.2 12.7 %collective-permute-start.8 = (bf16[128,1024]{1,0:T(8,128)(2,1)S(1)}, bf16[128,1024]{1,0:T(8,128)(2,1)S(1)}, u32[]{:S(2)}, u32[]{:S(2)}) collective-permute-start(bf16[128,1024]{1,0:T(8,128)(2,1)S(1)} %collective-permute-done.6.refs_1_.refs_7_), channel_id=1, source_target_pairs={{2,0},{4,6},{3,1},{5,7},{10,8},{12,14},{11,9},{13,15},{18,16},{20,... | collective-permute-start | bytes 786440 | tf_op jit(solution)/shard_map/ppermute | solution.py:387
  19.6 11.4 %collective-permute-start.9 = (bf16[128,1024]{1,0:T(8,128)(2,1)S(1)}, bf16[128,1024]{1,0:T(8,128)(2,1)S(1)}, u32[]{:S(2)}, u32[]{:S(2)}) collective-permute-start(bf16[128,1024]{1,0:T(8,128)(2,1)S(1)} %collective-permute-done.5.refs_0_.refs_5_), channel_id=1, source_target_pairs={{2,4},{4,2},{3,5},{5,3},{10,12},{12,10},{11,13},{13,11},{18,20},{2... | collective-permute-start | bytes 786440 | tf_op jit(solution)/shard_map/ppermute | solution.py:387
  21.9 10.4 %copy-start.2 = (f32[1024]{0:T(1024)S(1)}, f32[1024]{0:T(1024)}, u32[]{:S(2)}) copy-start(f32[1024]{0:T(1024)} %param.9) | copy-start | bytes 12292
  22.0 10.4 %copy-start.3 = (f32[512]{0:T(512)S(1)}, f32[512]{0:T(512)}, u32[]{:S(2)}) copy-start(f32[512]{0:T(512)} %param.8) | copy-start | bytes 6148
  23.8 2.7 %collective-permute-start = (s32[2,12]{1,0:T(2,128)S(1)}, s32[2,12]{1,0:T(2,128)S(1)}, u32[]{:S(2)}, u32[]{:S(2)}) collective-permute-start(s32[2,12]{1,0:T(2,128)S(1)} %copy-done), channel_id=1, source_target_pairs={{0,1},{1,0},{2,3},{3,2},{4,5},{5,4},{6,7},{7,6},{8,9},{9,8},{10,11... | collective-permute-start | bytes 296 | tf_op jit(solution)/shard_map/ppermute | solution.py:404
  25.3 16.1 %collective-permute-start.11 = (bf16[128,1024]{1,0:T(8,128)(2,1)S(1)}, bf16[128,1024]{1,0:T(8,128)(2,1)S(1)}, u32[]{:S(2)}, u32[]{:S(2)}) collective-permute-start(bf16[128,1024]{1,0:T(8,128)(2,1)S(1)} %collective-permute-done.2.refs_0_), channel_id=1, source_target_pairs={{2,0},{4,6},{3,1},{5,7},{10,8},{12,14},{11,9},{13,15},{18,16},{20,... | collective-permute-start | bytes 786440 | tf_op jit(solution)/shard_map/ppermute | solution.py:387
  31.0 11.9 %collective-permute-start.10 = (bf16[128,1024]{1,0:T(8,128)(2,1)S(1)}, bf16[128,1024]{1,0:T(8,128)(2,1)S(1)}, u32[]{:S(2)}, u32[]{:S(2)}) collective-permute-start(bf16[128,1024]{1,0:T(8,128)(2,1)S(1)} %collective-permute-done.9.refs_1_), channel_id=1, source_target_pairs={{2,0},{4,6},{3,1},{5,7},{10,8},{12,14},{11,9},{13,15},{18,16},{20,... | collective-permute-start | bytes 786440 | tf_op jit(solution)/shard_map/ppermute | solution.py:387

commit v2 on v1

--- a/solution.py
+++ b/solution.py
@@ -400,11 +400,12 @@
         marks.append(mark)
         return held
 
-    other = lax.ppermute(integrals, "rep", swap_rep)
     chosen_other = lax.ppermute(cd_tiles, "rep", swap_rep)
+    *own, tiles, chosen_other = lax.optimization_barrier((*own, integrals, chosen_other))
+    other = lax.ppermute(tiles, "rep", swap_rep)
     near, mid = send(own, swap_near), send(own, swap_mid)
     n_entry = integrals.shape[1]
-    taken, extra = range(n_entry * 8 // 12), range(n_entry * 8 // 12, n_entry)
+    taken, extra = range(n_entry), range(n_entry, n_entry)
     mine0, mark, _, _ = tile_sums(vir, cd_tiles, cd_tiles, integrals, 0, taken, None, per, (near[0], mid[0]))
     near[1], mid[1] = after(mark, near[1], mid[1])
     far, mid_out = send(near, swap_mid), send(mid, outward)

time: 43.5 us -> 43.3 us (level)
  the two profiles are of different devices: /device:TPU:17 before, /device:TPU:18 now
where the time goes in v2:
time: 43.3 us; the launch traced here: 43.5 us
  Pallas kernels  19.3 us (45%)
  starting transfers between devices  18.3 us (42%)
  waiting for transfers between devices  3.87 us (9%)
  local copies, waits for them, and re-layouts  1.75 us (4%)
    ppermute x10, starting transfers between devices, send(): return [lax.ppermute(piece, 'vir', pairs) for piece in pieces]  18 us
    pallas_call x2, Pallas kernels, tile_sums(): pl.pallas_call(functools.partial(sums_kernel, a=a, taken=taken, extra=ext...  9 us
    pallas_call x1, Pallas kernels, early_products(): pl.pallas_call(functools.partial(early_kernel, extra=extra), in_specs=[sm...  8.76 us
    ppermute x10, waiting for transfers between devices, send(): return [lax.ppermute(piece, 'vir', pairs) for piece in pieces]  3.59 us
    pallas_call x2, Pallas kernels, last_product(): pl.pallas_call(functools.partial(last_kernel, piece=piece), in_specs=[vme...  1.57 us
    dynamic_slice x1, local copies, waits for them, and re-layouts, dense_local(): lax.dynamic_slice_in_dim(amplitudes, rep_index * rows + i * piece, piece, 0)  1.06 us
  transfers between devices with their start and end apart: 12, of which 4 were waited for; matrix products, arithmetic and copies ran while one was open for 2% of the time, Pallas kernels for 44%

profile of v2, /device:TPU:18, one launch (start us, length us, event | category | flops | bytes accessed | tf_op | source)
XLA Modules:
  0.0 43.5 jit_solution(3620965533030566837)
XLA Ops:
  0.0 0.0 collective-permute-start
  0.0 1.1 %constant_dynamic-slice_fusion = (bf16[128,1024]{1,0:T(8,128)(2,1)S(1)}, bf16[128,1024]{1,0:T(8,128)(2,1)S(1)}) fusion(bf16[512,1024]{1,0:T(8,128)(2,1)} %param.5, s32[]{:T(128)S(6)} %select_n.7, s32[]{:T(128)S(6)} %select_n.6), kind=kLoop, calls=%fused_computation | loop fusion | bytes 1048584 | tf_op jit(solution)/shard_map/dynamic_slice | solution.py:391
  1.1 0.3 collective-permute-done.other_ref
  1.4 0.3 collective-permute-start.7
  1.7 1.6 %collective-permute-start.1 = (bf16[128,1024]{1,0:T(8,128)(2,1)S(1)}, bf16[128,1024]{1,0:T(8,128)(2,1)S(1)}, u32[]{:S(2)}, u32[]{:S(2)}) collective-permute-start(bf16[128,1024]{1,0:T(8,128)(2,1)S(1)} %get-tuple-element.29.refs_2_), channel_id=1, source_target_pairs={{0,2},{2,0},{4,6},{6,4},{1,3},{3,1},{5,7},{7,5},{8,10},{10,8},{12,... | collective-permute-start | bytes 786440 | tf_op jit(solution)/shard_map/ppermute | solution.py:387
  3.2 1.9 %collective-permute-start.3 = (bf16[128,1024]{1,0:T(8,128)(2,1)S(1)}, bf16[128,1024]{1,0:T(8,128)(2,1)S(1)}, u32[]{:S(2)}, u32[]{:S(2)}) collective-permute-start(bf16[128,1024]{1,0:T(8,128)(2,1)S(1)} %get-tuple-element.29.refs_2_), channel_id=1, source_target_pairs={{2,4},{4,2},{3,5},{5,3},{10,12},{12,10},{11,13},{13,11},{18,20},{2... | collective-permute-start | bytes 786440 | tf_op jit(solution)/shard_map/ppermute | solution.py:387
  5.1 0.1 collective-permute-start.5
  5.2 3.9 %collective-permute-start.6 = (bf16[128,1024]{1,0:T(8,128)(2,1)S(1)}, bf16[128,1024]{1,0:T(8,128)(2,1)S(1)}, u32[]{:S(2)}, u32[]{:S(2)}) collective-permute-start(bf16[128,1024]{1,0:T(8,128)(2,1)S(1)} %get-tuple-element.30.refs_3_), channel_id=1, source_target_pairs={{2,4},{4,2},{3,5},{5,3},{10,12},{12,10},{11,13},{13,11},{18,20},{2... | collective-permute-start | bytes 786440 | tf_op jit(solution)/shard_map/ppermute | solution.py:387
  9.2 1.6 %collective-permute-done.1.refs_0_.refs_4_ = bf16[128,1024]{1,0:T(8,128)(2,1)S(1)} collective-permute-done((bf16[128,1024]{1,0:T(8,128)(2,1)S(1)}, bf16[128,1024]{1,0:T(8,128)(2,1)S(1)}, u32[]{:S(2)}, u32[]{:S(2)}) %collective-permute-start.1) | collective-permute-done | bytes 262176 | tf_op jit(solution)/shard_map/ppermute | solution.py:387
  10.8 2.3 %collective-permute-start.2 = (bf16[128,1024]{1,0:T(8,128)(2,1)S(1)}, bf16[128,1024]{1,0:T(8,128)(2,1)S(1)}, u32[]{:S(2)}, u32[]{:S(2)}) collective-permute-start(bf16[128,1024]{1,0:T(8,128)(2,1)S(1)} %collective-permute-done.1.refs_0_.refs_4_), channel_id=1, source_target_pairs={{2,4},{4,2},{3,5},{5,3},{10,12},{12,10},{11,13},{13,11},{18,20},{2... | collective-permute-start | bytes 786440 | tf_op jit(solution)/shard_map/ppermute | solution.py:387
  13.2 1.1 %collective-permute-done.3.refs_1_.refs_6_ = bf16[128,1024]{1,0:T(8,128)(2,1)S(1)} collective-permute-done((bf16[128,1024]{1,0:T(8,128)(2,1)S(1)}, bf16[128,1024]{1,0:T(8,128)(2,1)S(1)}, u32[]{:S(2)}, u32[]{:S(2)}) %collective-permute-start.3) | collective-permute-done | bytes 262176 | tf_op jit(solution)/shard_map/ppermute | solution.py:387
  14.3 1.3 %collective-permute-start.4 = (bf16[128,1024]{1,0:T(8,128)(2,1)S(1)}, bf16[128,1024]{1,0:T(8,128)(2,1)S(1)}, u32[]{:S(2)}, u32[]{:S(2)}) collective-permute-start(bf16[128,1024]{1,0:T(8,128)(2,1)S(1)} %collective-permute-done.3.refs_1_.refs_6_), channel_id=1, source_target_pairs={{2,0},{4,6},{3,1},{5,7},{10,8},{12,14},{11,9},{13,15},{18,16},{20,... | collective-permute-start | bytes 786440 | tf_op jit(solution)/shard_map/ppermute | solution.py:387
  15.6 0.0 copy-start
  15.6 0.7 %copy-done = s32[2,12]{1,0:T(2,128)S(1)} copy-done((s32[2,12]{1,0:T(2,128)S(1)}, s32[2,12]{1,0:T(2,128)}, u32[]{:S(2)}) %copy-start) | copy-done | bytes 120
  16.3 4.5 %shard_map.55 = (bf16[4,2,512,512]{3,2,1,0:T(8,128)(2,1)S(1)}, bf16[16,128]{1,0:T(8,128)(2,1)S(1)}, s32[1]{0:T(128)}, s32[8]{0:T(128)}) custom-call(s32[1]{0:T(128)} %bitcast.vir_ref, s32[2,12]{1,0:T(2,128)S(1)} %copy-done, s32[2,12]{1,0:T(2,128)S(1)} %copy-done, bf16[2,12,512,512]{3,2,1,0:T(8,128)(2,1)} %refs_1_.1, ...), custom_call_target="tpu_custom_call" | custom-call | bytes 1000000 | tf_op jit(solution)/shard_map/pallas_call | solution.py:179
  20.8 0.0 collective-permute-done.5.refs_0_.refs_5_
  20.8 1.3 %collective-permute-start.8 = (bf16[128,1024]{1,0:T(8,128)(2,1)S(1)}, bf16[128,1024]{1,0:T(8,128)(2,1)S(1)}, u32[]{:S(2)}, u32[]{:S(2)}) collective-permute-start(bf16[128,1024]{1,0:T(8,128)(2,1)S(1)} %collective-permute-done.6.refs_1_.refs_7_), channel_id=1, source_target_pairs={{2,0},{4,6},{3,1},{5,7},{10,8},{12,14},{11,9},{13,15},{18,16},{20,... | collective-permute-start | bytes 786440 | tf_op jit(solution)/shard_map/ppermute | solution.py:387
  22.1 2.3 %collective-permute-start.9 = (bf16[128,1024]{1,0:T(8,128)(2,1)S(1)}, bf16[128,1024]{1,0:T(8,128)(2,1)S(1)}, u32[]{:S(2)}, u32[]{:S(2)}) collective-permute-start(bf16[128,1024]{1,0:T(8,128)(2,1)S(1)} %collective-permute-done.5.refs_0_.refs_5_), channel_id=1, source_target_pairs={{2,4},{4,2},{3,5},{5,3},{10,12},{12,10},{11,13},{13,11},{18,20},{2... | collective-permute-start | bytes 786440 | tf_op jit(solution)/shard_map/ppermute | solution.py:387
  24.4 0.0 copy-start.2
  24.5 0.0 copy-start.3
  24.5 0.0 collective-permute-done.2.refs_0_
  24.5 0.0 collective-permute-done.4.refs_1_.refs_8_
  24.5 1.3 %collective-permute-start.11 = (bf16[128,1024]{1,0:T(8,128)(2,1)S(1)}, bf16[128,1024]{1,0:T(8,128)(2,1)S(1)}, u32[]{:S(2)}, u32[]{:S(2)}) collective-permute-start(bf16[128,1024]{1,0:T(8,128)(2,1)S(1)} %collective-permute-done.2.refs_0_), channel_id=1, source_target_pairs={{2,0},{4,6},{3,1},{5,7},{10,8},{12,14},{11,9},{13,15},{18,16},{20,... | collective-permute-start | bytes 786440 | tf_op jit(solution)/shard_map/ppermute | solution.py:387
  25.8 4.5 %shard_map.57 = (bf16[4,2,512,512]{3,2,1,0:T(8,128)(2,1)S(1)}, bf16[16,128]{1,0:T(8,128)(2,1)S(1)}, s32[16]{0:T(128)S(1)}, s32[192]{0:T(256)S(1)}) custom-call(s32[1]{0:T(128)} %bitcast.vir_ref, s32[2,12]{1,0:T(2,128)S(1)} %copy-done.1, s32[2,12]{1,0:T(2,128)S(1)} %collective-permute-done.other_ref, bf16[2,12,512,512]{3,2,1,0:T(8,128)(2,1)} %refs_1_.1, ...), custom_call_target="tpu_custom_call" | custom-call | bytes 1000000 | tf_op jit(solution)/shard_map/pallas_call | solution.py:179
  30.3 0.0 collective-permute-done.8.refs_9_.refs_0_
  30.3 0.8 %collective-permute-done.9.refs_1_ = bf16[128,1024]{1,0:T(8,128)(2,1)S(1)} collective-permute-done((bf16[128,1024]{1,0:T(8,128)(2,1)S(1)}, bf16[128,1024]{1,0:T(8,128)(2,1)S(1)}, u32[]{:S(2)}, u32[]{:S(2)}) %collective-permute-start.9) | collective-permute-done | bytes 262176 | tf_op jit(solution)/shard_map/ppermute | solution.py:387
  31.1 2.0 %collective-permute-start.10 = (bf16[128,1024]{1,0:T(8,128)(2,1)S(1)}, bf16[128,1024]{1,0:T(8,128)(2,1)S(1)}, u32[]{:S(2)}, u32[]{:S(2)}) collective-permute-start(bf16[128,1024]{1,0:T(8,128)(2,1)S(1)} %collective-permute-done.9.refs_1_), channel_id=1, source_target_pairs={{2,0},{4,6},{3,1},{5,7},{10,8},{12,14},{11,9},{13,15},{18,16},{20,... | collective-permute-start | bytes 786440 | tf_op jit(solution)/shard_map/ppermute | solution.py:387
  33.1 0.0 collective-permute-done.7.refs_0_
  33.1 8.8 %shard_map.58 = (f32[2,256,512]{2,1,0:T(8,128)S(1)}, bf16[2,2,512,512]{3,2,1,0:T(8,128)(2,1)S(1)}, f32[8,128]{1,0:T(8,128)S(1)}) custom-call(s32[1]{0:T(128)} %bitcast.vir_ref, s32[1]{0:T(128)} %bitcast.1.rep_ref, s32[16]{0:T(128)S(1)} %get-tuple-element.36.count_ref, s32[192]{0:T(256)S(1)} %get-tuple-element.37.entry_ref, f32[1,512]{1,0:T(1,128)S(1)} %bitcast.5, ...), custom_call_target="tpu_custom_call" | custom-call | flops 2147483648 | bytes 12582912 | tf_op jit(solution)/shard_map/pallas_call | solution.py:288
  41.9 0.0 collective-permute-done.11.refs_2_
  41.9 1.5 %shard_map.60.refs_3_ = bf16[256,1024]{1,0:T(8,128)(2,1)} custom-call(f32[2,256,512]{2,1,0:T(8,128)S(1)} %get-tuple-element.43.total_ref, bf16[2,2,512,512]{3,2,1,0:T(8,128)(2,1)S(1)} %get-tuple-element.44.sums_ref, f32[8,128]{1,0:T(8,128)S(1)} %get-tuple-element.45.inner_ref, bf16[128,1024]{1,0:T(8,128)(2,1)S(1)} %collective-permute-done.2.refs_0_, ...), custom_call_target="tpu_custom_call" | custom-call | bytes 1000000 | tf_op jit(solution)/shard_map/pallas_call | solution.py:365
  43.4 0.1 shard_map.61
  (8 shorter events, 0.0 us)
Async XLA Ops:
  0.0 1.4 %collective-permute-start = (s32[2,12]{1,0:T(2,128)}, s32[2,12]{1,0:T(2,128)S(1)}, u32[]{:S(2)}, u32[]{:S(2)}) collective-permute-start(s32[2,12]{1,0:T(2,128)} %chosen_ref.3), channel_id=1, source_target_pairs={{0,1},{1,0},{2,3},{3,2},{4,5},{5,4},{6,7},{7,6},{8,9},{9,8},{10,11... | collective-permute-start | bytes 296 | tf_op jit(solution)/shard_map/ppermute | solution.py:403
  1.4 31.8 %collective-permute-start.7 = (bf16[2,12,512,512]{3,2,1,0:T(8,128)(2,1)}, bf16[2,12,512,512]{3,2,1,0:T(8,128)(2,1)}, u32[]{:S(2)}, u32[]{:S(2)}) collective-permute-start(bf16[2,12,512,512]{3,2,1,0:T(8,128)(2,1)} %refs_1_.1), channel_id=1, source_target_pairs={{0,1},{1,0},{2,3},{3,2},{4,5},{5,4},{6,7},{7,6},{8,9},{9,8},{10,11... | collective-permute-start | bytes 37748744 | tf_op jit(solution)/shard_map/ppermute | solution.py:405
  1.7 9.1 %collective-permute-start.1 = (bf16[128,1024]{1,0:T(8,128)(2,1)S(1)}, bf16[128,1024]{1,0:T(8,128)(2,1)S(1)}, u32[]{:S(2)}, u32[]{:S(2)}) collective-permute-start(bf16[128,1024]{1,0:T(8,128)(2,1)S(1)} %get-tuple-element.29.refs_2_), channel_id=1, source_target_pairs={{0,2},{2,0},{4,6},{6,4},{1,3},{3,1},{5,7},{7,5},{8,10},{10,8},{12,... | collective-permute-start | bytes 786440 | tf_op jit(solution)/shard_map/ppermute | solution.py:387
  3.2 11.1 %collective-permute-start.3 = (bf16[128,1024]{1,0:T(8,128)(2,1)S(1)}, bf16[128,1024]{1,0:T(8,128)(2,1)S(1)}, u32[]{:S(2)}, u32[]{:S(2)}) collective-permute-start(bf16[128,1024]{1,0:T(8,128)(2,1)S(1)} %get-tuple-element.29.refs_2_), channel_id=1, source_target_pairs={{2,4},{4,2},{3,5},{5,3},{10,12},{12,10},{11,13},{13,11},{18,20},{2... | collective-permute-start | bytes 786440 | tf_op jit(solution)/shard_map/ppermute | solution.py:387
  5.1 15.6 %collective-permute-start.5 = (bf16[128,1024]{1,0:T(8,128)(2,1)S(1)}, bf16[128,1024]{1,0:T(8,128)(2,1)S(1)}, u32[]{:S(2)}, u32[]{:S(2)}) collective-permute-start(bf16[128,1024]{1,0:T(8,128)(2,1)S(1)} %get-tuple-element.30.refs_3_), channel_id=1, source_target_pairs={{0,2},{2,0},{4,6},{6,4},{1,3},{3,1},{5,7},{7,5},{8,10},{10,8},{12,... | collective-permute-start | bytes 786440 | tf_op jit(solution)/shard_map/ppermute | solution.py:387
  5.2 15.6 %collective-permute-start.6 = (bf16[128,1024]{1,0:T(8,128)(2,1)S(1)}, bf16[128,1024]{1,0:T(8,128)(2,1)S(1)}, u32[]{:S(2)}, u32[]{:S(2)}) collective-permute-start(bf16[128,1024]{1,0:T(8,128)(2,1)S(1)} %get-tuple-element.30.refs_3_), channel_id=1, source_target_pairs={{2,4},{4,2},{3,5},{5,3},{10,12},{12,10},{11,13},{13,11},{18,20},{2... | collective-permute-start | bytes 786440 | tf_op jit(solution)/shard_map/ppermute | solution.py:387
  10.8 13.7 %collective-permute-start.2 = (bf16[128,1024]{1,0:T(8,128)(2,1)S(1)}, bf16[128,1024]{1,0:T(8,128)(2,1)S(1)}, u32[]{:S(2)}, u32[]{:S(2)}) collective-permute-start(bf16[128,1024]{1,0:T(8,128)(2,1)S(1)} %collective-permute-done.1.refs_0_.refs_4_), channel_id=1, source_target_pairs={{2,4},{4,2},{3,5},{5,3},{10,12},{12,10},{11,13},{13,11},{18,20},{2... | collective-permute-start | bytes 786440 | tf_op jit(solution)/shard_map/ppermute | solution.py:387
  14.3 10.2 %collective-permute-start.4 = (bf16[128,1024]{1,0:T(8,128)(2,1)S(1)}, bf16[128,1024]{1,0:T(8,128)(2,1)S(1)}, u32[]{:S(2)}, u32[]{:S(2)}) collective-permute-start(bf16[128,1024]{1,0:T(8,128)(2,1)S(1)} %collective-permute-done.3.refs_1_.refs_6_), channel_id=1, source_target_pairs={{2,0},{4,6},{3,1},{5,7},{10,8},{12,14},{11,9},{13,15},{18,16},{20,... | collective-permute-start | bytes 786440 | tf_op jit(solution)/shard_map/ppermute | solution.py:387
  15.6 0.7 %copy-start = (s32[2,12]{1,0:T(2,128)S(1)}, s32[2,12]{1,0:T(2,128)}, u32[]{:S(2)}) copy-start(s32[2,12]{1,0:T(2,128)} %chosen_ref.3) | copy-start | bytes 292
  16.3 9.5 %copy-start.1 = (s32[2,12]{1,0:T(2,128)S(1)}, s32[2,12]{1,0:T(2,128)}, u32[]{:S(2)}) copy-start(s32[2,12]{1,0:T(2,128)} %chosen_ref.3) | copy-start | bytes 292
  20.8 9.5 %collective-permute-start.8 = (bf16[128,1024]{1,0:T(8,128)(2,1)S(1)}, bf16[128,1024]{1,0:T(8,128)(2,1)S(1)}, u32[]{:S(2)}, u32[]{:S(2)}) collective-permute-start(bf16[128,1024]{1,0:T(8,128)(2,1)S(1)} %collective-permute-done.6.refs_1_.refs_7_), channel_id=1, source_target_pairs={{2,0},{4,6},{3,1},{5,7},{10,8},{12,14},{11,9},{13,15},{18,16},{20,... | collective-permute-start | bytes 786440 | tf_op jit(solution)/shard_map/ppermute | solution.py:387
  22.1 9.0 %collective-permute-start.9 = (bf16[128,1024]{1,0:T(8,128)(2,1)S(1)}, bf16[128,1024]{1,0:T(8,128)(2,1)S(1)}, u32[]{:S(2)}, u32[]{:S(2)}) collective-permute-start(bf16[128,1024]{1,0:T(8,128)(2,1)S(1)} %collective-permute-done.5.refs_0_.refs_5_), channel_id=1, source_target_pairs={{2,4},{4,2},{3,5},{5,3},{10,12},{12,10},{11,13},{13,11},{18,20},{2... | collective-permute-start | bytes 786440 | tf_op jit(solution)/shard_map/ppermute | solution.py:387
  24.4 8.7 %copy-start.2 = (f32[1024]{0:T(1024)S(1)}, f32[1024]{0:T(1024)}, u32[]{:S(2)}) copy-start(f32[1024]{0:T(1024)} %param.9) | copy-start | bytes 12292
  24.5 8.7 %copy-start.3 = (f32[512]{0:T(512)S(1)}, f32[512]{0:T(512)}, u32[]{:S(2)}) copy-start(f32[512]{0:T(512)} %param.8) | copy-start | bytes 6148
  24.5 17.4 %collective-permute-start.11 = (bf16[128,1024]{1,0:T(8,128)(2,1)S(1)}, bf16[128,1024]{1,0:T(8,128)(2,1)S(1)}, u32[]{:S(2)}, u32[]{:S(2)}) collective-permute-start(bf16[128,1024]{1,0:T(8,128)(2,1)S(1)} %collective-permute-done.2.refs_0_), channel_id=1, source_target_pairs={{2,0},{4,6},{3,1},{5,7},{10,8},{12,14},{11,9},{13,15},{18,16},{20,... | collective-permute-start | bytes 786440 | tf_op jit(solution)/shard_map/ppermute | solution.py:387
  31.1 12.3 %collective-permute-start.10 = (bf16[128,1024]{1,0:T(8,128)(2,1)S(1)}, bf16[128,1024]{1,0:T(8,128)(2,1)S(1)}, u32[]{:S(2)}, u32[]{:S(2)}) collective-permute-start(bf16[128,1024]{1,0:T(8,128)(2,1)S(1)} %collective-permute-done.9.refs_1_), channel_id=1, source_target_pairs={{2,0},{4,6},{3,1},{5,7},{10,8},{12,14},{11,9},{13,15},{18,16},{20,... | collective-permute-start | bytes 786440 | tf_op jit(solution)/shard_map/ppermute | solution.py:387

commit v3 on v2

--- a/solution.py
+++ b/solution.py
@@ -311,6 +311,26 @@
     refs[-1][...] = jnp.zeros_like(refs[-1])
 
 
+def near_by_kernel(array_ref, *refs):
+    copy_ref, there_ref = refs[-2:]
+    copy_ref[...] = array_ref[...]
+    there_ref[...] = jnp.zeros_like(there_ref)
+
+
+def near_by(array, *first):
+    vmem = pl.BlockSpec(memory_space=pltpu.VMEM)
+    return pl.pallas_call(
+        near_by_kernel,
+        in_specs=[vmem] + [pl.BlockSpec(memory_space=pl.ANY)] * len(first),
+        out_specs=[vmem] * 2,
+        out_shape=[
+            jax.ShapeDtypeStruct(array.shape, array.dtype), jax.ShapeDtypeStruct((16, 128), jnp.bfloat16)
+        ],
+        compiler_params=pltpu.CompilerParams(vmem_limit_bytes=MIB),
+        cost_estimate=pl.CostEstimate(flops=0, bytes_accessed=1000000, transcendentals=0),
+    )(array, *first)
+
+
 def all_there(*arrays):
     return pl.pallas_call(
         there_kernel,
@@ -404,14 +424,16 @@
     *own, tiles, chosen_other = lax.optimization_barrier((*own, integrals, chosen_other))
     other = lax.ppermute(tiles, "rep", swap_rep)
     near, mid = send(own, swap_near), send(own, swap_mid)
+    chosen, mark = near_by(cd_tiles, own[0], chosen_other)
+    near[0], = after(mark, near[0])
     n_entry = integrals.shape[1]
-    taken, extra = range(n_entry), range(n_entry, n_entry)
-    mine0, mark, _, _ = tile_sums(vir, cd_tiles, cd_tiles, integrals, 0, taken, None, per, (near[0], mid[0]))
+    taken, extra = range(n_entry * 8 // 12), range(n_entry * 8 // 12, n_entry)
+    mine0, mark, _, _ = tile_sums(vir, chosen, chosen, integrals, 0, taken, None, per, (near[0], mid[0]))
     near[1], mid[1] = after(mark, near[1], mid[1])
     far, mid_out = send(near, swap_mid), send(mid, outward)
     far[0], mid_out[0] = after(all_there(near[1], mid[1]), far[0], mid_out[0])
     mine1, mark, count, entry = tile_sums(
-        vir, cd_tiles, chosen_other, integrals, 1, range(n_entry), extra, per, (far[0], mid_out[0])
+        vir, chosen, chosen_other, integrals, 1, range(n_entry), extra, per, (far[0], mid_out[0])
     )
     mid_out[1], = after(mark, mid_out[1])
     far[1], = after(all_there(mid_out[1]), far[1])

time: 43.3 us -> 43.5 us (level)
  waiting for transfers between devices: 3.87 us -> 4.99 us
  starting transfers between devices: 18.3 us -> 17.2 us
    ppermute x10, waiting for transfers between devices: 3.59 us -> 4.71 us  [send(): return [lax.ppermute(piece, 'vir', pairs) for piece in pieces]]
    ppermute x10, starting transfers between devices: 18 us -> 16.9 us  [send(): return [lax.ppermute(piece, 'vir', pairs) for piece in pieces]]
    pallas_call x2, Pallas kernels: 9 us -> 8.06 us  [tile_sums(): pl.pallas_call(functools.partial(sums_kernel, a=a, taken=taken, extra=ext...]
    pallas_call x1, Pallas kernels: 8.76 us -> 9.58 us  [early_products(): pl.pallas_call(functools.partial(early_kernel, extra=extra), in_specs=[sm...]
  transfers between devices with their start and end apart: 12 -> 12, of which waited for: 4 -> 5; matrix products, arithmetic and copies ran while one was open for 2% -> 2% of each run, Pallas kernels for 44% -> 44%
where the time goes in v3:
time: 43.5 us; the launch traced here: 43.4 us
  Pallas kernels  19.2 us (44%)
  starting transfers between devices  17.2 us (40%)
  waiting for transfers between devices  4.99 us (11%)
  local copies, waits for them, and re-layouts  1.75 us (4%)
    ppermute x10, starting transfers between devices, send(): return [lax.ppermute(piece, 'vir', pairs) for piece in pieces]  16.9 us
    pallas_call x1, Pallas kernels, early_products(): pl.pallas_call(functools.partial(early_kernel, extra=extra), in_specs=[sm...  9.58 us
    pallas_call x2, Pallas kernels, tile_sums(): pl.pallas_call(functools.partial(sums_kernel, a=a, taken=taken, extra=ext...  8.06 us
    ppermute x10, waiting for transfers between devices, send(): return [lax.ppermute(piece, 'vir', pairs) for piece in pieces]  4.71 us
    pallas_call x2, Pallas kernels, last_product(): pl.pallas_call(functools.partial(last_kernel, piece=piece), in_specs=[vme...  1.57 us
    dynamic_slice x1, local copies, waits for them, and re-layouts, dense_local(): lax.dynamic_slice_in_dim(amplitudes, rep_index * rows + i * piece, piece, 0)  1.06 us
  transfers between devices with their start and end apart: 12, of which 5 were waited for; matrix products, arithmetic and copies ran while one was open for 2% of the time, Pallas kernels for 44%

profile of v3, /device:TPU:18, one launch (start us, length us, event | category | flops | bytes accessed | tf_op | source)
XLA Modules:
  0.0 43.4 jit_solution(17331836690124096920)
XLA Ops:
  0.0 0.0 collective-permute-start
  0.0 1.1 %constant_dynamic-slice_fusion = (bf16[128,1024]{1,0:T(8,128)(2,1)S(1)}, bf16[128,1024]{1,0:T(8,128)(2,1)S(1)}) fusion(bf16[512,1024]{1,0:T(8,128)(2,1)} %param.5, s32[]{:T(128)S(6)} %select_n.7, s32[]{:T(128)S(6)} %select_n.6), kind=kLoop, calls=%fused_computation | loop fusion | bytes 1048584 | tf_op jit(solution)/shard_map/dynamic_slice | solution.py:411
  1.1 0.3 collective-permute-done.refs_1_.other_ref
  1.4 0.3 collective-permute-start.7
  1.7 1.6 %collective-permute-start.1 = (bf16[128,1024]{1,0:T(8,128)(2,1)S(1)}, bf16[128,1024]{1,0:T(8,128)(2,1)S(1)}, u32[]{:S(2)}, u32[]{:S(2)}) collective-permute-start(bf16[128,1024]{1,0:T(8,128)(2,1)S(1)} %get-tuple-element.32.refs_0_.refs_2_), channel_id=1, source_target_pairs={{0,2},{2,0},{4,6},{6,4},{1,3},{3,1},{5,7},{7,5},{8,10},{10,8},{12,... | collective-permute-start | bytes 786440 | tf_op jit(solution)/shard_map/ppermute | solution.py:407
  3.2 1.9 %collective-permute-start.3 = (bf16[128,1024]{1,0:T(8,128)(2,1)S(1)}, bf16[128,1024]{1,0:T(8,128)(2,1)S(1)}, u32[]{:S(2)}, u32[]{:S(2)}) collective-permute-start(bf16[128,1024]{1,0:T(8,128)(2,1)S(1)} %get-tuple-element.32.refs_0_.refs_2_), channel_id=1, source_target_pairs={{2,4},{4,2},{3,5},{5,3},{10,12},{12,10},{11,13},{13,11},{18,20},{2... | collective-permute-start | bytes 786440 | tf_op jit(solution)/shard_map/ppermute | solution.py:407
  5.1 0.1 collective-permute-start.5
  5.2 3.9 %collective-permute-start.6 = (bf16[128,1024]{1,0:T(8,128)(2,1)S(1)}, bf16[128,1024]{1,0:T(8,128)(2,1)S(1)}, u32[]{:S(2)}, u32[]{:S(2)}) collective-permute-start(bf16[128,1024]{1,0:T(8,128)(2,1)S(1)} %get-tuple-element.37.refs_3_), channel_id=1, source_target_pairs={{2,4},{4,2},{3,5},{5,3},{10,12},{12,10},{11,13},{13,11},{18,20},{2... | collective-permute-start | bytes 786440 | tf_op jit(solution)/shard_map/ppermute | solution.py:407
  9.2 0.0 copy-start.2
  9.2 0.7 %copy-done.2 = s32[2,12]{1,0:T(2,128)S(1)} copy-done((s32[2,12]{1,0:T(2,128)S(1)}, s32[2,12]{1,0:T(2,128)}, u32[]{:S(2)}) %copy-start.2) | copy-done | bytes 120
  9.8 1.0 %collective-permute-done.1.refs_0_.refs_4_ = bf16[128,1024]{1,0:T(8,128)(2,1)S(1)} collective-permute-done((bf16[128,1024]{1,0:T(8,128)(2,1)S(1)}, bf16[128,1024]{1,0:T(8,128)(2,1)S(1)}, u32[]{:S(2)}, u32[]{:S(2)}) %collective-permute-start.1) | collective-permute-done | bytes 262176 | tf_op jit(solution)/shard_map/ppermute | solution.py:407
  10.8 2.3 %collective-permute-start.2 = (bf16[128,1024]{1,0:T(8,128)(2,1)S(1)}, bf16[128,1024]{1,0:T(8,128)(2,1)S(1)}, u32[]{:S(2)}, u32[]{:S(2)}) collective-permute-start(bf16[128,1024]{1,0:T(8,128)(2,1)S(1)} %collective-permute-done.1.refs_0_.refs_4_), channel_id=1, source_target_pairs={{2,4},{4,2},{3,5},{5,3},{10,12},{12,10},{11,13},{13,11},{18,20},{2... | collective-permute-start | bytes 786440 | tf_op jit(solution)/shard_map/ppermute | solution.py:407
  13.2 1.1 %collective-permute-done.3.refs_1_.refs_6_ = bf16[128,1024]{1,0:T(8,128)(2,1)S(1)} collective-permute-done((bf16[128,1024]{1,0:T(8,128)(2,1)S(1)}, bf16[128,1024]{1,0:T(8,128)(2,1)S(1)}, u32[]{:S(2)}, u32[]{:S(2)}) %collective-permute-start.3) | collective-permute-done | bytes 262176 | tf_op jit(solution)/shard_map/ppermute | solution.py:407
  14.3 1.3 %collective-permute-start.4 = (bf16[128,1024]{1,0:T(8,128)(2,1)S(1)}, bf16[128,1024]{1,0:T(8,128)(2,1)S(1)}, u32[]{:S(2)}, u32[]{:S(2)}) collective-permute-start(bf16[128,1024]{1,0:T(8,128)(2,1)S(1)} %collective-permute-done.3.refs_1_.refs_6_), channel_id=1, source_target_pairs={{2,0},{4,6},{3,1},{5,7},{10,8},{12,14},{11,9},{13,15},{18,16},{20,... | collective-permute-start | bytes 786440 | tf_op jit(solution)/shard_map/ppermute | solution.py:407
  15.6 3.7 %shard_map.56 = (bf16[4,2,512,512]{3,2,1,0:T(8,128)(2,1)S(1)}, bf16[16,128]{1,0:T(8,128)(2,1)S(1)}, s32[1]{0:T(128)}, s32[8]{0:T(128)}) custom-call(s32[1]{0:T(128)} %bitcast.vir_ref, s32[2,12]{1,0:T(2,128)S(1)} %get-tuple-element.34.chosen_ref.other_ref, s32[2,12]{1,0:T(2,128)S(1)} %get-tuple-element.34.chosen_ref.other_ref, ...), custom_call_target="tpu_custom_call" | custom-call | bytes 1000000 | tf_op jit(solution)/shard_map/pallas_call | solution.py:179
  19.3 0.0 collective-permute-done.5.refs_0_.refs_5_
  19.3 0.6 %collective-permute-done.6.refs_1_.refs_7_ = bf16[128,1024]{1,0:T(8,128)(2,1)S(1)} collective-permute-done((bf16[128,1024]{1,0:T(8,128)(2,1)S(1)}, bf16[128,1024]{1,0:T(8,128)(2,1)S(1)}, u32[]{:S(2)}, u32[]{:S(2)}) %collective-permute-start.6) | collective-permute-done | bytes 262176 | tf_op jit(solution)/shard_map/ppermute | solution.py:407
  19.9 1.3 %collective-permute-start.8 = (bf16[128,1024]{1,0:T(8,128)(2,1)S(1)}, bf16[128,1024]{1,0:T(8,128)(2,1)S(1)}, u32[]{:S(2)}, u32[]{:S(2)}) collective-permute-start(bf16[128,1024]{1,0:T(8,128)(2,1)S(1)} %collective-permute-done.6.refs_1_.refs_7_), channel_id=1, source_target_pairs={{2,0},{4,6},{3,1},{5,7},{10,8},{12,14},{11,9},{13,15},{18,16},{20,... | collective-permute-start | bytes 786440 | tf_op jit(solution)/shard_map/ppermute | solution.py:407
  21.2 1.9 %collective-permute-start.9 = (bf16[128,1024]{1,0:T(8,128)(2,1)S(1)}, bf16[128,1024]{1,0:T(8,128)(2,1)S(1)}, u32[]{:S(2)}, u32[]{:S(2)}) collective-permute-start(bf16[128,1024]{1,0:T(8,128)(2,1)S(1)} %collective-permute-done.5.refs_0_.refs_5_), channel_id=1, source_target_pairs={{2,4},{4,2},{3,5},{5,3},{10,12},{12,10},{11,13},{13,11},{18,20},{2... | collective-permute-start | bytes 786440 | tf_op jit(solution)/shard_map/ppermute | solution.py:407
  23.2 0.0 copy-start
  23.2 0.0 copy-start.1
  23.2 2.0 %collective-permute-done.2.refs_0_ = bf16[128,1024]{1,0:T(8,128)(2,1)S(1)} collective-permute-done((bf16[128,1024]{1,0:T(8,128)(2,1)S(1)}, bf16[128,1024]{1,0:T(8,128)(2,1)S(1)}, u32[]{:S(2)}, u32[]{:S(2)}) %collective-permute-start.2) | collective-permute-done | bytes 262176 | tf_op jit(solution)/shard_map/ppermute | solution.py:407
  25.2 0.0 collective-permute-done.4.refs_1_.refs_8_
  25.2 1.3 %collective-permute-start.11 = (bf16[128,1024]{1,0:T(8,128)(2,1)S(1)}, bf16[128,1024]{1,0:T(8,128)(2,1)S(1)}, u32[]{:S(2)}, u32[]{:S(2)}) collective-permute-start(bf16[128,1024]{1,0:T(8,128)(2,1)S(1)} %collective-permute-done.2.refs_0_), channel_id=1, source_target_pairs={{2,0},{4,6},{3,1},{5,7},{10,8},{12,14},{11,9},{13,15},{18,16},{20,... | collective-permute-start | bytes 786440 | tf_op jit(solution)/shard_map/ppermute | solution.py:407
  26.5 4.4 %shard_map.58 = (bf16[4,2,512,512]{3,2,1,0:T(8,128)(2,1)S(1)}, bf16[16,128]{1,0:T(8,128)(2,1)S(1)}, s32[16]{0:T(128)S(1)}, s32[256]{0:T(256)S(1)}) custom-call(s32[1]{0:T(128)} %bitcast.vir_ref, s32[2,12]{1,0:T(2,128)S(1)} %get-tuple-element.34.chosen_ref.other_ref, s32[2,12]{1,0:T(2,128)S(1)} %collective-permute-done.refs_1_.other_ref, ...), custom_call_target="tpu_custom_call" | custom-call | bytes 1000000 | tf_op jit(solution)/shard_map/pallas_call | solution.py:179
  30.9 0.0 collective-permute-done.8.refs_9_.refs_0_
  30.9 1.3 %collective-permute-start.10 = (bf16[128,1024]{1,0:T(8,128)(2,1)S(1)}, bf16[128,1024]{1,0:T(8,128)(2,1)S(1)}, u32[]{:S(2)}, u32[]{:S(2)}) collective-permute-start(bf16[128,1024]{1,0:T(8,128)(2,1)S(1)} %collective-permute-done.9.refs_1_), channel_id=1, source_target_pairs={{2,0},{4,6},{3,1},{5,7},{10,8},{12,14},{11,9},{13,15},{18,16},{20,... | collective-permute-start | bytes 786440 | tf_op jit(solution)/shard_map/ppermute | solution.py:407
  32.2 0.0 collective-permute-done.7.refs_0_
  32.2 9.6 %shard_map.59 = (f32[2,256,512]{2,1,0:T(8,128)S(1)}, bf16[2,2,512,512]{3,2,1,0:T(8,128)(2,1)S(1)}, f32[8,128]{1,0:T(8,128)S(1)}) custom-call(s32[1]{0:T(128)} %bitcast.vir_ref, s32[1]{0:T(128)} %bitcast.1.rep_ref, s32[16]{0:T(128)S(1)} %get-tuple-element.43.count_ref, s32[256]{0:T(256)S(1)} %get-tuple-element.44.entry_ref, f32[1,512]{1,0:T(1,128)S(1)} %bitcast.5, ...), custom_call_target="tpu_custom_call" | custom-call | flops 2147483648 | bytes 12582912 | tf_op jit(solution)/shard_map/pallas_call | solution.py:288
  41.8 0.0 collective-permute-done.11.refs_2_
  41.8 1.5 %shard_map.61.refs_3_ = bf16[256,1024]{1,0:T(8,128)(2,1)} custom-call(f32[2,256,512]{2,1,0:T(8,128)S(1)} %get-tuple-element.50.total_ref, bf16[2,2,512,512]{3,2,1,0:T(8,128)(2,1)S(1)} %get-tuple-element.51.sums_ref, f32[8,128]{1,0:T(8,128)S(1)} %get-tuple-element.52.inner_ref, bf16[128,1024]{1,0:T(8,128)(2,1)S(1)} %collective-permute-done.2.refs_0_, ...), custom_call_target="tpu_custom_call" | custom-call | bytes 1000000 | tf_op jit(solution)/shard_map/pallas_call | solution.py:385
  43.3 0.1 shard_map.62
  (7 shorter events, 0.0 us)
Async XLA Ops:
  0.0 1.4 %collective-permute-start = (s32[2,12]{1,0:T(2,128)}, s32[2,12]{1,0:T(2,128)S(1)}, u32[]{:S(2)}, u32[]{:S(2)}) collective-permute-start(s32[2,12]{1,0:T(2,128)} %array_ref.1), channel_id=1, source_target_pairs={{0,1},{1,0},{2,3},{3,2},{4,5},{5,4},{6,7},{7,6},{8,9},{9,8},{10,11... | collective-permute-start | bytes 296 | tf_op jit(solution)/shard_map/ppermute | solution.py:423
  1.4 30.8 %collective-permute-start.7 = (bf16[2,12,512,512]{3,2,1,0:T(8,128)(2,1)}, bf16[2,12,512,512]{3,2,1,0:T(8,128)(2,1)}, u32[]{:S(2)}, u32[]{:S(2)}) collective-permute-start(bf16[2,12,512,512]{3,2,1,0:T(8,128)(2,1)} %refs_1_.1), channel_id=1, source_target_pairs={{0,1},{1,0},{2,3},{3,2},{4,5},{5,4},{6,7},{7,6},{8,9},{9,8},{10,11... | collective-permute-start | bytes 37748744 | tf_op jit(solution)/shard_map/ppermute | solution.py:425
  1.7 9.1 %collective-permute-start.1 = (bf16[128,1024]{1,0:T(8,128)(2,1)S(1)}, bf16[128,1024]{1,0:T(8,128)(2,1)S(1)}, u32[]{:S(2)}, u32[]{:S(2)}) collective-permute-start(bf16[128,1024]{1,0:T(8,128)(2,1)S(1)} %get-tuple-element.32.refs_0_.refs_2_), channel_id=1, source_target_pairs={{0,2},{2,0},{4,6},{6,4},{1,3},{3,1},{5,7},{7,5},{8,10},{10,8},{12,... | collective-permute-start | bytes 786440 | tf_op jit(solution)/shard_map/ppermute | solution.py:407
  3.2 11.1 %collective-permute-start.3 = (bf16[128,1024]{1,0:T(8,128)(2,1)S(1)}, bf16[128,1024]{1,0:T(8,128)(2,1)S(1)}, u32[]{:S(2)}, u32[]{:S(2)}) collective-permute-start(bf16[128,1024]{1,0:T(8,128)(2,1)S(1)} %get-tuple-element.32.refs_0_.refs_2_), channel_id=1, source_target_pairs={{2,4},{4,2},{3,5},{5,3},{10,12},{12,10},{11,13},{13,11},{18,20},{2... | collective-permute-start | bytes 786440 | tf_op jit(solution)/shard_map/ppermute | solution.py:407
  5.1 14.2 %collective-permute-start.5 = (bf16[128,1024]{1,0:T(8,128)(2,1)S(1)}, bf16[128,1024]{1,0:T(8,128)(2,1)S(1)}, u32[]{:S(2)}, u32[]{:S(2)}) collective-permute-start(bf16[128,1024]{1,0:T(8,128)(2,1)S(1)} %get-tuple-element.37.refs_3_), channel_id=1, source_target_pairs={{0,2},{2,0},{4,6},{6,4},{1,3},{3,1},{5,7},{7,5},{8,10},{10,8},{12,... | collective-permute-start | bytes 786440 | tf_op jit(solution)/shard_map/ppermute | solution.py:407
  5.2 14.7 %collective-permute-start.6 = (bf16[128,1024]{1,0:T(8,128)(2,1)S(1)}, bf16[128,1024]{1,0:T(8,128)(2,1)S(1)}, u32[]{:S(2)}, u32[]{:S(2)}) collective-permute-start(bf16[128,1024]{1,0:T(8,128)(2,1)S(1)} %get-tuple-element.37.refs_3_), channel_id=1, source_target_pairs={{2,4},{4,2},{3,5},{5,3},{10,12},{12,10},{11,13},{13,11},{18,20},{2... | collective-permute-start | bytes 786440 | tf_op jit(solution)/shard_map/ppermute | solution.py:407
  9.2 0.7 %copy-start.2 = (s32[2,12]{1,0:T(2,128)S(1)}, s32[2,12]{1,0:T(2,128)}, u32[]{:S(2)}) copy-start(s32[2,12]{1,0:T(2,128)} %array_ref.1) | copy-start | bytes 292
  10.8 14.4 %collective-permute-start.2 = (bf16[128,1024]{1,0:T(8,128)(2,1)S(1)}, bf16[128,1024]{1,0:T(8,128)(2,1)S(1)}, u32[]{:S(2)}, u32[]{:S(2)}) collective-permute-start(bf16[128,1024]{1,0:T(8,128)(2,1)S(1)} %collective-permute-done.1.refs_0_.refs_4_), channel_id=1, source_target_pairs={{2,4},{4,2},{3,5},{5,3},{10,12},{12,10},{11,13},{13,11},{18,20},{2... | collective-permute-start | bytes 786440 | tf_op jit(solution)/shard_map/ppermute | solution.py:407
  14.3 10.9 %collective-permute-start.4 = (bf16[128,1024]{1,0:T(8,128)(2,1)S(1)}, bf16[128,1024]{1,0:T(8,128)(2,1)S(1)}, u32[]{:S(2)}, u32[]{:S(2)}) collective-permute-start(bf16[128,1024]{1,0:T(8,128)(2,1)S(1)} %collective-permute-done.3.refs_1_.refs_6_), channel_id=1, source_target_pairs={{2,0},{4,6},{3,1},{5,7},{10,8},{12,14},{11,9},{13,15},{18,16},{20,... | collective-permute-start | bytes 786440 | tf_op jit(solution)/shard_map/ppermute | solution.py:407
  19.9 10.9 %collective-permute-start.8 = (bf16[128,1024]{1,0:T(8,128)(2,1)S(1)}, bf16[128,1024]{1,0:T(8,128)(2,1)S(1)}, u32[]{:S(2)}, u32[]{:S(2)}) collective-permute-start(bf16[128,1024]{1,0:T(8,128)(2,1)S(1)} %collective-permute-done.6.refs_1_.refs_7_), channel_id=1, source_target_pairs={{2,0},{4,6},{3,1},{5,7},{10,8},{12,14},{11,9},{13,15},{18,16},{20,... | collective-permute-start | bytes 786440 | tf_op jit(solution)/shard_map/ppermute | solution.py:407
  21.2 9.7 %collective-permute-start.9 = (bf16[128,1024]{1,0:T(8,128)(2,1)S(1)}, bf16[128,1024]{1,0:T(8,128)(2,1)S(1)}, u32[]{:S(2)}, u32[]{:S(2)}) collective-permute-start(bf16[128,1024]{1,0:T(8,128)(2,1)S(1)} %collective-permute-done.5.refs_0_.refs_5_), channel_id=1, source_target_pairs={{2,4},{4,2},{3,5},{5,3},{10,12},{12,10},{11,13},{13,11},{18,20},{2... | collective-permute-start | bytes 786440 | tf_op jit(solution)/shard_map/ppermute | solution.py:407
  23.2 9.1 %copy-start = (f32[1024]{0:T(1024)S(1)}, f32[1024]{0:T(1024)}, u32[]{:S(2)}) copy-start(f32[1024]{0:T(1024)} %param.9) | copy-start | bytes 12292
  23.2 9.1 %copy-start.1 = (f32[512]{0:T(512)S(1)}, f32[512]{0:T(512)}, u32[]{:S(2)}) copy-start(f32[512]{0:T(512)} %param.8) | copy-start | bytes 6148
  25.2 16.6 %collective-permute-start.11 = (bf16[128,1024]{1,0:T(8,128)(2,1)S(1)}, bf16[128,1024]{1,0:T(8,128)(2,1)S(1)}, u32[]{:S(2)}, u32[]{:S(2)}) collective-permute-start(bf16[128,1024]{1,0:T(8,128)(2,1)S(1)} %collective-permute-done.2.refs_0_), channel_id=1, source_target_pairs={{2,0},{4,6},{3,1},{5,7},{10,8},{12,14},{11,9},{13,15},{18,16},{20,... | collective-permute-start | bytes 786440 | tf_op jit(solution)/shard_map/ppermute | solution.py:407
  30.9 12.4 %collective-permute-start.10 = (bf16[128,1024]{1,0:T(8,128)(2,1)S(1)}, bf16[128,1024]{1,0:T(8,128)(2,1)S(1)}, u32[]{:S(2)}, u32[]{:S(2)}) collective-permute-start(bf16[128,1024]{1,0:T(8,128)(2,1)S(1)} %collective-permute-done.9.refs_1_), channel_id=1, source_target_pairs={{2,0},{4,6},{3,1},{5,7},{10,8},{12,14},{11,9},{13,15},{18,16},{20,... | collective-permute-start | bytes 786440 | tf_op jit(solution)/shard_map/ppermute | solution.py:407
